TPU v7x, 256 devices: a whole 4x4x8 slice. The times are simulated.
256 devices in a mesh: row: 8 (over x, core), col: 32 (over z, y).
Axes of the slice: x: 4, y: 4, z: 8, core: 2. Of those that a mesh axis runs over, the one named last changes fastest.
Arguments:
- tangent: bfloat16 [32, 131072], P(None, ('col', 'row')), may hold values from -180 to 180
- activity: bfloat16 [131072], P(('col', 'row')), may hold values from -5 to 5
- block_keys: int32 [8, 512], P('row', 'col'), may hold values from 0 to 1073741823
Outputs:
- tangent_new: float32 [32, 131072], P(None, ('row', 'col'))
- next_state: float32 [131072], P(('row', 'col'))
- r_factor: float32 [32, 32], replicated
- first_factor: float32 [32, 32], replicated
All inputs are finite; a program needn't handle non-finite values.
Results may differ from a plain program's by a relative error of at most 0.0006.
Values may be sent and summed in bfloat16 or wider, within the bound.
No kernel may reach another device: no remote copies, remote signals or barrier semaphores. Data moves between devices by JAX's collectives and lax.ppermute only.
A program may use at most 64 MiB of HBM per device.

v0:
```python
import functools
import math

import jax
import jax.numpy as jnp
from jax import lax
from jax.experimental import pallas as pl
from jax.experimental.pallas import tpu as pltpu
from jax.sharding import Mesh
from jax.sharding import PartitionSpec as P

N = 131072
VECS = 32
PAD = 48
KEYCOLS = 256
X, CORE, Z, Y = 4, 2, 8, 4
OWN = N // (X * CORE * Z * Y)
ROWS = OWN * Y
SEG = OWN * X * CORE
GROUP = 32
SPARE = 40
SENT = 40
GRAM_ROW = 36
LANES = 512
KEYS = SEG // KEYCOLS
GRAM_TILE = 4 * (KEYS // 8)
SCALE = 2.0 / math.sqrt(5461.25 * N)
HIGH = lax.Precision.HIGHEST
PARAMS = pltpu.CompilerParams(vmem_limit_bytes=16 * 2**20)
STEP = 16
VMEM = pl.BlockSpec(memory_space=pltpu.VMEM)
SMEM = pl.BlockSpec(memory_space=pltpu.SMEM)


def shift_right(value, amount):
    return lax.shift_right_logical(value, jnp.full(value.shape, amount, jnp.int32))


def coupling(value):
    value = value ^ shift_right(value, 15)
    value = value * jnp.int32(739982445)
    value = value ^ shift_right(value, 13)
    value = value * jnp.int32(695872825)
    value = value ^ shift_right(value, 16)
    return (value.astype(jnp.int8) ^ jnp.int8(-128)).astype(jnp.bfloat16)


def spare_tile(block_ref, tile):
    return block_ref[SPARE - 8 : SPARE + 8, 128 * tile : 128 * tile + 128].astype(jnp.float32)[8:]


def block_kernel(keys_ref, *refs):
    pair_refs, block_ref = refs[:X], refs[X]
    wide = CORE * OWN
    for shift in range(X):
        chip = lax.rem(lax.axis_index("x") + X - shift, X)
        block_ref[:, pl.ds(pl.multiple_of(chip * wide, wide), wide)] = pair_refs[shift][...]
    own = block_ref[:VECS, :]
    gram = lax.dot_general(own, own, (((1,), (1,)), ((), ())), preferred_element_type=jnp.float32)
    rest = pack_gram(gram / N)
    rows = lax.broadcasted_iota(jnp.int32, (8, 128), 0)
    parts = []
    for part in range(KEYS // 8):
        keys = jnp.zeros((8, 128), jnp.int32)
        for row in range(8):
            keys = jnp.where(rows == row, keys_ref[0, part * 8 + row], keys)
        parts.append(keys)
    tiles = []
    for digit in range(4):
        for keys in parts:
            tiles.append(jnp.bitwise_and(shift_right(keys, 8 * digit), 255).astype(jnp.float32))
    for _ in range(3):
        part = rest.astype(jnp.bfloat16).astype(jnp.float32)
        tiles.append(part)
        rest = rest - part
    for k, tile in enumerate(tiles):
        lanes = slice(128 * k, 128 * k + 128)
        above = block_ref[SPARE - 8 : SPARE + 8, lanes].astype(jnp.float32)[:8]
        block_ref[SPARE - 8 : SPARE + 8, lanes] = jnp.concatenate((above, tile)).astype(jnp.bfloat16)


def drive_kernel(*refs, shifts, earlier, last):
    blocks = len(shifts)
    block_refs = refs[:blocks]
    earlier_refs = refs[blocks : blocks + 2 * earlier]
    *out_refs, grams_ref, total_ref, vectors_ref, bases_ref = refs[blocks + 2 * earlier :]
    groups = SEG // GROUP

    for slot in range(Z):
        grams_ref[slot] = earlier_refs[1][slot] if earlier else jnp.zeros((8, 128), jnp.float32)
    steps = lax.broadcasted_iota(jnp.int32, (8, 128), 0) * jnp.int32(GROUP)
    for k, shift in enumerate(shifts):
        place = lax.rem(lax.axis_index("z") + (Z + shift), Z)
        vectors_ref[k] = block_refs[k][...]
        gram = jnp.zeros((8, 128), jnp.float32)
        for part in range(3):
            gram = gram + spare_tile(block_refs[k], GRAM_TILE + part)
        grams_ref[place] = gram
        first_column = (place * Y + lax.axis_index("y")) * SEG
        for part in range(KEYS // 8):
            keys = jnp.zeros((8, 128), jnp.int32)
            for digit in range(4):
                tile = spare_tile(block_refs[k], digit * (KEYS // 8) + part)
                keys = keys + tile.astype(jnp.int32) * jnp.int32(256**digit)
            for row in range(8):
                key = part * 8 + row
                columns = first_column + key * KEYCOLS + steps
                at = k * groups + key * 8
                bases_ref[at : at + 8, :] = keys[row : row + 1] + columns * jnp.int32(668265261)

    first_row = (lax.axis_index("x") * CORE + lax.axis_index("core")) * (N // (X * CORE)) + lax.axis_index("z") * ROWS
    row_at = lax.broadcasted_iota(jnp.int32, (GROUP, 128), 1)
    spread = lax.broadcasted_iota(jnp.int32, (GROUP, 128), 0) * jnp.int32(668265261)

    def lanes_body(part, carry):
        lane = pl.multiple_of(part * LANES, LANES)
        starts = [
            (first_row + lane + 128 * k + row_at) * jnp.int32(374761393) + spread
            for k in range(LANES // 128)
        ]

        def body(number, total):
            first = pl.multiple_of(number * groups, groups)
            parts = []
            for group in range(groups):
                base = bases_ref[pl.ds(first + group, 1), :]
                parts.append(jnp.concatenate([coupling(base + start) for start in starts], axis=1))
            return total + jnp.dot(
                vectors_ref[number],
                jnp.concatenate(parts, axis=0),
                preferred_element_type=jnp.float32,
            )

        here = pl.ds(lane, LANES)
        initial = earlier_refs[0][:, here] if earlier else jnp.zeros((PAD, LANES), jnp.float32)
        total_ref[:, here] = lax.fori_loop(0, blocks, body, initial)
        return carry

    lax.fori_loop(0, ROWS // LANES, lanes_body, 0)
    if not last:
        out_refs[0][...] = total_ref[...]
        return
    gram = grams_ref[0]
    for slot in range(1, Z):
        gram = gram + grams_ref[slot]
    for shift, out_ref in enumerate(out_refs):
        to = lax.rem(lax.axis_index("y") + shift, Y)
        out_ref[...] = total_ref[:SENT, pl.ds(pl.multiple_of(to * OWN, OWN), OWN)]
        out_ref[GRAM_ROW:, :128] = gram[:4]
        out_ref[GRAM_ROW:, 128:256] = gram[4:]


def partial_drive(shifts, blocks, earlier=(), last=False):
    count = len(blocks)
    drive = jax.ShapeDtypeStruct((PAD, ROWS), jnp.float32)
    if last:
        out_shape = [jax.ShapeDtypeStruct((SENT, OWN), jnp.float32)] * Y
    else:
        out_shape = [drive]
    grams = jax.ShapeDtypeStruct((Z, 8, 128), jnp.float32)
    return pl.pallas_call(
        functools.partial(drive_kernel, shifts=shifts, earlier=len(earlier) // 2, last=last),
        in_specs=[VMEM] * (count + len(earlier)),
        out_specs=[VMEM] * (len(out_shape) + 1),
        out_shape=out_shape + [grams],
        scratch_shapes=[
            pltpu.VMEM(drive.shape, jnp.float32),
            pltpu.VMEM((count, PAD, SEG), jnp.bfloat16),
            pltpu.VMEM((count * SEG // GROUP, 128), jnp.int32),
        ],
        cost_estimate=pl.CostEstimate(
            flops=count * SEG * ROWS * 1500, bytes_accessed=count * PAD * SEG * 2, transcendentals=0
        ),
        compiler_params=PARAMS,
    )(*blocks, *earlier)


def pack_gram(gram):
    return jnp.concatenate([gram[8 * k : 8 * k + 8] for k in range(4)], axis=1)


def unpack_gram(packed):
    return jnp.concatenate([packed[:, 32 * k : 32 * k + 32] for k in range(4)], axis=0)


def gram_of(rows):
    return lax.dot_general(
        rows, rows, (((1,), (1,)), ((), ())), precision=HIGH, preferred_element_type=jnp.float32
    ) / N


def dot(left, right):
    return jnp.dot(left, right, precision=HIGH, preferred_element_type=jnp.float32)


def factor(gram, floor=0.0):
    rows = lax.broadcasted_iota(jnp.int32, (VECS, VECS), 0)
    columns = lax.broadcasted_iota(jnp.int32, (VECS, VECS), 1)
    wide = (VECS, 2 * VECS)
    row_at = lax.broadcasted_iota(jnp.int32, wide, 0)
    work = jnp.concatenate((gram, (rows == columns).astype(jnp.float32)), axis=1)
    scales = jnp.zeros(wide, jnp.float32)
    for first in range(0, VECS, STEP):
        spread = [
            jnp.broadcast_to(work[:, first + k : first + k + 1], wide) for k in range(STEP)
        ]
        ratios = []
        for k in range(STEP):
            at = first + k
            column = spread[k]
            for m in range(k):
                element = jnp.broadcast_to(column[first + m : first + m + 1], wide)
                column = column - ratios[m] * element
            pivot = jnp.broadcast_to(column[at : at + 1], wide)
            if floor:
                least = jnp.maximum(floor * gram[at : at + 1, at : at + 1], 1e-30)
                pivot = jnp.maximum(pivot, least)
            ratios.append(jnp.where(row_at > at, column / pivot, 0.0))
            scales = jnp.where(row_at == at, lax.rsqrt(pivot), scales)
        for k in range(STEP):
            work = work - ratios[k] * jnp.broadcast_to(work[first + k : first + k + 1], wide)
    diagonal = jnp.where(rows == columns, 1.0 / scales[:, :VECS], 0.0)
    work = work * scales
    upper = jnp.where(rows < columns, work[:, :VECS], diagonal)
    return upper, work[:, VECS:]


def first_kernel(mine_ref, others_ref, *refs):
    others_ref, refs = (others_ref, *refs[: Y - 2]), refs[Y - 2 :]
    state_ref, scaled_ref, gram_ref, upper_ref, inputs_ref = refs
    drive = mine_ref[...]

    def gram_part(piece):
        return jnp.concatenate((piece[GRAM_ROW:, :128], piece[GRAM_ROW:, 128:256]))

    inputs_ref[lax.axis_index("y")] = gram_part(drive)
    for shift, other_ref in enumerate(others_ref, 1):
        other = other_ref[...]
        drive = drive + other
        inputs_ref[lax.rem(lax.axis_index("y") + (Y - shift), Y)] = gram_part(other)
    state = jnp.tanh(SCALE * drive[VECS : VECS + 1])
    grown = (SCALE * (1.0 - state * state)) * drive[:VECS]
    inputs = inputs_ref[0]
    for k in range(1, Y):
        inputs = inputs + inputs_ref[k]
    upper, inverse = factor(unpack_gram(inputs), 1e-6)
    scaled = dot(inverse, grown)
    state_ref[...] = state
    scaled_ref[...] = scaled
    gram_ref[...] = jnp.broadcast_to(pack_gram(gram_of(scaled)), gram_ref.shape)
    upper_ref[...] = upper


def second_kernel(grams_ref, scaled_ref, input_upper_ref, result_ref, product_ref, upper_ref):
    gram = unpack_gram(jnp.sum(grams_ref[...], axis=0))
    near_upper, inverse = factor(gram)
    first = dot(inverse, scaled_ref[...])
    upper = dot(near_upper, input_upper_ref[...])
    gram_two = lax.dot_general(
        dot(inverse, gram),
        inverse,
        (((1,), (1,)), ((), ())),
        precision=HIGH,
        preferred_element_type=jnp.float32,
    )
    second_upper, second_inverse = factor(gram_two)
    result_ref[...] = dot(second_inverse, first)
    product_ref[...] = dot(second_upper, upper)
    upper_ref[...] = upper


def gather_grams(copies):
    near = jnp.sum(lax.all_to_all(copies, ("x", "core", "y"), 0, 0), axis=0)
    return lax.all_to_all(jnp.broadcast_to(near, (Z, *near.shape)), "z", 0, 0)


def per_device(tangent, activity, block_keys):
    own = jnp.concatenate(
        (tangent, activity.reshape(1, -1), jnp.zeros((PAD - VECS - 1, OWN), jnp.bfloat16)), axis=0
    )
    other = lax.ppermute(own, "core", [(0, 1), (1, 0)])
    pair = jnp.where(
        lax.axis_index("core") == 0,
        jnp.concatenate((own, other), axis=1),
        jnp.concatenate((other, own), axis=1),
    )
    pairs = [pair] + [
        lax.ppermute(pair, "x", [(i, (i + shift) % X) for i in range(X)]) for shift in range(1, X)
    ]
    near = pl.pallas_call(
        block_kernel,
        in_specs=[SMEM] + [VMEM] * X,
        out_shape=jax.ShapeDtypeStruct((PAD, SEG), jnp.bfloat16),
        compiler_params=PARAMS,
    )(block_keys, *pairs)

    up = [(i, (i + 1) % Z) for i in range(Z)]
    down = [(i, (i - 1) % Z) for i in range(Z)]
    below, above = lax.ppermute(near, "z", up), lax.ppermute(near, "z", down)
    earlier = partial_drive((0,), [near])
    for step in range(1, Z // 2):
        next_below = lax.ppermute(below, "z", up)
        next_above = lax.ppermute(above, "z", down) if step + 1 < Z // 2 else None
        earlier = partial_drive((-step, step), [below, above], earlier)
        below, above = next_below, next_above
    *pieces, _ = partial_drive((Z // 2,), [below], earlier, last=True)
    for shift in range(1, Y):
        pieces[shift] = lax.ppermute(pieces[shift], "y", [(i, (i + shift) % Y) for i in range(Y)])

    square = jax.ShapeDtypeStruct((VECS, VECS), jnp.float32)
    wide = jax.ShapeDtypeStruct((VECS, OWN), jnp.float32)
    state, scaled, gram, input_upper = pl.pallas_call(
        first_kernel,
        out_shape=(
            jax.ShapeDtypeStruct((1, OWN), jnp.float32),
            wide,
            jax.ShapeDtypeStruct((X * CORE * Y, 8, 128), jnp.float32),
            square,
        ),
        compiler_params=PARAMS,
        scratch_shapes=[pltpu.VMEM((Y, 8, 128), jnp.float32)],
    )(*pieces)
    result, product, upper = pl.pallas_call(
        second_kernel, out_shape=(wide, square, square), compiler_params=PARAMS
    )(gather_grams(gram), scaled, input_upper)
    return result, state.reshape(OWN), product, upper


def solution(mesh):
    split = Mesh(mesh.devices.reshape(X, CORE, Z, Y), ("x", "core", "z", "y"))
    columns, rows = ("z", "y", "x", "core"), ("x", "core", "z", "y")
    return jax.shard_map(
        per_device,
        mesh=split,
        in_specs=(P(None, columns), P(columns), P(("x", "core"), ("z", "y"))),
        out_specs=(P(None, rows), P(rows), P(), P()),
        check_vma=False,
    )
```

profile of v0, /device:TPU:1, one launch (start us, length us, event | category | flops | bytes accessed | tf_op | source)
XLA Modules:
  0.0 164.2 jit_solution(3480885644048731837)
XLA Ops:
  2.2 3.3 %collective-permute-start = (bf16[48,512]{1,0:T(8,128)(2,1)S(1)}, bf16[48,512]{1,0:T(8,128)(2,1)S(1)}, u32[]{:S(2)}, u32[]{:S(2)}) collective-permute-start(bf16[48,512]{1,0:T(8,128)(2,1)S(1)} %pad_maximum_fusion), channel_id=1, source_target_pairs={{0,32},{32,0},{1,33},{33,1},{2,34},{34,2},{3,35},{35,3},{4,36},{36... | collective-permute-start | bytes 147464 | tf_op jit(solution)/shard_map/ppermute | solution.py:281
  5.5 0.9 collective-permute-done
  6.5 1.9 %collective-permute-start.2 = (bf16[48,1024]{1,0:T(8,128)(2,1)S(1)}, bf16[48,1024]{1,0:T(8,128)(2,1)S(1)}, u32[]{:S(2)}, u32[]{:S(2)}) collective-permute-start(bf16[48,1024]{1,0:T(8,128)(2,1)S(1)} %maximum_select_fusion.refs_0_), channel_id=1, source_target_pairs={{0,128},{64,192},{128,0},{192,64},{1,129},{65,193},{129,1},{193,65... | collective-permute-start | bytes 294920 | tf_op jit(solution)/shard_map/ppermute | solution.py:288
  8.4 1.2 collective-permute-start.3
  9.6 3.1 %collective-permute-done.1.refs_1_ = bf16[48,1024]{1,0:T(8,128)(2,1)S(1)} collective-permute-done((bf16[48,1024]{1,0:T(8,128)(2,1)S(1)}, bf16[48,1024]{1,0:T(8,128)(2,1)S(1)}, u32[]{:S(2)}, u32[]{:S(2)}) %collective-permute-start.1) | collective-permute-done | bytes 98336 | tf_op jit(solution)/shard_map/ppermute | solution.py:288
  13.1 1.0 collective-permute-done.3.refs_3_
  14.1 0.9 shard_map.66.refs_0_
  15.6 4.0 %collective-permute-start.8 = (bf16[48,4096]{1,0:T(8,128)(2,1)S(1)}, bf16[48,4096]{1,0:T(8,128)(2,1)S(1)}, u32[]{:S(2)}, u32[]{:S(2)}) collective-permute-start(bf16[48,4096]{1,0:T(8,128)(2,1)S(1)} %shard_map.66.refs_0_), channel_id=1, source_target_pairs={{0,28},{4,0},{8,4},{12,8},{16,12},{20,16},{24,20},{28,24},{1,29},{... | collective-permute-start | bytes 1179656 | tf_op jit(solution)/shard_map/ppermute | solution.py:299
  19.7 12.0 %shard_map.67 = (f32[48,2048]{1,0:T(8,128)S(1)}, f32[8,8,128]{2,1,0:T(8,128)S(1)}) custom-call(bf16[48,4096]{1,0:T(8,128)(2,1)S(1)} %shard_map.66.refs_0_), custom_call_target="tpu_custom_call" | custom-call | flops 12582912000 | bytes 393216 | tf_op jit(solution)/shard_map/pallas_call | solution.py:161
  31.8 2.7 %collective-permute-start.9 = (bf16[48,4096]{1,0:T(8,128)(2,1)S(1)}, bf16[48,4096]{1,0:T(8,128)(2,1)S(1)}, u32[]{:S(2)}, u32[]{:S(2)}) collective-permute-start(bf16[48,4096]{1,0:T(8,128)(2,1)S(1)} %collective-permute-done.8.refs_1_), channel_id=1, source_target_pairs={{0,28},{4,0},{8,4},{12,8},{16,12},{20,16},{24,20},{28,24},{1,29},{... | collective-permute-start | bytes 1179656 | tf_op jit(solution)/shard_map/ppermute | solution.py:303
  34.4 24.0 %shard_map.68 = (f32[48,2048]{1,0:T(8,128)S(1)}, f32[8,8,128]{2,1,0:T(8,128)S(1)}) custom-call(bf16[48,4096]{1,0:T(8,128)(2,1)S(1)} %collective-permute-done.4.refs_0_, bf16[48,4096]{1,0:T(8,128)(2,1)S(1)} %collective-permute-done.8.refs_1_, f32[48,2048]{1,0:T(8,128)S(1)} %get-tuple-element.23.refs_2_, f32[8,8,128]{2,1,0:T(8,128)S(1)} %get-tuple-element.24.refs_3_), custom_call_target="tpu_custom_call" | custom-call | flops 25165824000 | bytes 786432 | tf_op jit(solution)/shard_map/pallas_call | solution.py:161
  58.5 2.7 %collective-permute-start.10 = (bf16[48,4096]{1,0:T(8,128)(2,1)S(1)}, bf16[48,4096]{1,0:T(8,128)(2,1)S(1)}, u32[]{:S(2)}, u32[]{:S(2)}) collective-permute-start(bf16[48,4096]{1,0:T(8,128)(2,1)S(1)} %collective-permute-done.9.refs_1_), channel_id=1, source_target_pairs={{0,28},{4,0},{8,4},{12,8},{16,12},{20,16},{24,20},{28,24},{1,29},{... | collective-permute-start | bytes 1179656 | tf_op jit(solution)/shard_map/ppermute | solution.py:303
  61.1 24.0 %shard_map.69 = (f32[48,2048]{1,0:T(8,128)S(1)}, f32[8,8,128]{2,1,0:T(8,128)S(1)}) custom-call(bf16[48,4096]{1,0:T(8,128)(2,1)S(1)} %collective-permute-done.5.refs_0_, bf16[48,4096]{1,0:T(8,128)(2,1)S(1)} %collective-permute-done.9.refs_1_, f32[48,2048]{1,0:T(8,128)S(1)} %get-tuple-element.25.refs_2_, f32[8,8,128]{2,1,0:T(8,128)S(1)} %get-tuple-element.26.refs_3_), custom_call_target="tpu_custom_call" | custom-call | flops 25165824000 | bytes 786432 | tf_op jit(solution)/shard_map/pallas_call | solution.py:161
  85.4 24.0 %shard_map.70 = (f32[48,2048]{1,0:T(8,128)S(1)}, f32[8,8,128]{2,1,0:T(8,128)S(1)}) custom-call(bf16[48,4096]{1,0:T(8,128)(2,1)S(1)} %collective-permute-done.6.refs_0_, bf16[48,4096]{1,0:T(8,128)(2,1)S(1)} %collective-permute-done.10.refs_1_, f32[48,2048]{1,0:T(8,128)S(1)} %get-tuple-element.27.refs_2_, f32[8,8,128]{2,1,0:T(8,128)S(1)} %get-tuple-element.28.refs_3_), custom_call_target="tpu_custom_call" | custom-call | flops 25165824000 | bytes 786432 | tf_op jit(solution)/shard_map/pallas_call | solution.py:161
  109.4 12.6 %shard_map.71 = (f32[40,512]{1,0:T(8,128)S(1)}, f32[40,512]{1,0:T(8,128)S(1)}, f32[40,512]{1,0:T(8,128)S(1)}, f32[40,512]{1,0:T(8,128)S(1)}, f32[8,8,128]{2,1,0:T(8,128)}) custom-call(bf16[48,4096]{1,0:T(8,128)(2,1)S(1)} %collective-permute-done.7.refs_0_, f32[48,2048]{1,0:T(8,128)S(1)} %get-tuple-element.29.refs_1_, f32[8,8,128]{2,1,0:T(8,128)S(1)} %get-tuple-element.30.refs_2_), custom_call_target="tpu_custom_call" | custom-call | flops 12582912000 | bytes 393216 | tf_op jit(solution)/shard_map/pallas_call | solution.py:161
  122.0 1.3 collective-permute-start.11
  123.3 2.6 %collective-permute-start.12 = (f32[40,512]{1,0:T(8,128)S(1)}, f32[40,512]{1,0:T(8,128)S(1)}, u32[]{:S(2)}, u32[]{:S(2)}) collective-permute-start(f32[40,512]{1,0:T(8,128)S(1)} %get-tuple-element.33), channel_id=1, source_target_pairs={{0,2},{1,3},{2,0},{3,1},{4,6},{5,7},{6,4},{7,5},{8,10},{9,11},{10,... | collective-permute-start | bytes 245768 | tf_op jit(solution)/shard_map/ppermute | solution.py:308
  125.9 1.1 collective-permute-start.13
  127.0 1.6 collective-permute-done.12.refs_0_
  128.6 0.9 collective-permute-done.13.refs_1_
  129.5 1.8 %shard_map.72 = (f32[1,512]{1,0:T(1,128)}, f32[32,512]{1,0:T(8,128)S(1)}, f32[32,8,128]{2,1,0:T(8,128)S(1)}, f32[32,32]{1,0:T(8,128)S(1)}) custom-call(f32[40,512]{1,0:T(8,128)S(1)} %get-tuple-element.31.mine_ref, f32[40,512]{1,0:T(8,128)S(1)} %collective-permute-done.11.others_ref, f32[40,512]{1,0:T(8,128)S(1)} %collective-permute-done.12.refs_0_, ...), custom_call_target="tpu_custom_call" | custom-call | tf_op jit(solution)/shard_map/pallas_call | solution.py:312
  131.3 17.4 %all_to_all.10 = f32[32,8,128]{2,1,0:T(8,128)S(1)} all-to-all(f32[32,8,128]{2,1,0:T(8,128)S(1)} %get-tuple-element.35), channel_id=1, replica_groups=mesh['x'=4,'core'=2,'z'=8,'y'=4] {'x','core','y'}, dimensions={0} | all-to-all | bytes 262144 | tf_op jit(solution)/shard_map/all_to_all | solution.py:273
  148.8 12.7 %all_to_all.11.grams_ref = f32[8,8,128]{2,1,0:T(8,128)S(1)} all-to-all(f32[8,8,128]{2,1,0:T(8,128)S(1)} %broadcast_in_dim.7), channel_id=1, replica_groups=mesh['x'=4,'core'=2,'z'=8,'y'=4] {'z'}, dimensions={0} | all-to-all | bytes 65536 | tf_op jit(solution)/shard_map/all_to_all | solution.py:274
  161.5 2.7 %shard_map.73 = (f32[32,512]{1,0:T(8,128)}, f32[32,32]{1,0:T(8,128)}, f32[32,32]{1,0:T(8,128)}) custom-call(f32[8,8,128]{2,1,0:T(8,128)S(1)} %all_to_all.11.grams_ref, f32[32,512]{1,0:T(8,128)S(1)} %get-tuple-element.36.scaled_ref, f32[32,32]{1,0:T(8,128)S(1)} %get-tuple-element.37.input_upper_ref), custom_call_target="tpu_custom_call" | custom-call | tf_op jit(solution)/shard_map/pallas_call | solution.py:323
  (24 shorter events, 3.3 us)
Async XLA Ops:
  1.3 5.1 %copy-start.1 = (bf16[32,512]{1,0:T(8,128)(2,1)S(1)}, bf16[32,512]{1,0:T(8,128)(2,1)}, u32[]{:S(2)}) copy-start(bf16[32,512]{1,0:T(8,128)(2,1)} %param.3) | copy-start | bytes 98308
  2.2 4.2 %collective-permute-start = (bf16[48,512]{1,0:T(8,128)(2,1)S(1)}, bf16[48,512]{1,0:T(8,128)(2,1)S(1)}, u32[]{:S(2)}, u32[]{:S(2)}) collective-permute-start(bf16[48,512]{1,0:T(8,128)(2,1)S(1)} %pad_maximum_fusion), channel_id=1, source_target_pairs={{0,32},{32,0},{1,33},{33,1},{2,34},{34,2},{3,35},{35,3},{4,36},{36... | collective-permute-start | bytes 147464 | tf_op jit(solution)/shard_map/ppermute | solution.py:281
  5.5 8.6 %copy-start = (s32[1,16]{1,0:T(1,128)S(1)}, s32[1,16]{1,0:T(1,128)}, u32[]{:S(2)}) copy-start(s32[1,16]{1,0:T(1,128)} %keys_ref.1) | copy-start | bytes 196
  6.4 6.2 %collective-permute-start.1 = (bf16[48,1024]{1,0:T(8,128)(2,1)S(1)}, bf16[48,1024]{1,0:T(8,128)(2,1)S(1)}, u32[]{:S(2)}, u32[]{:S(2)}) collective-permute-start(bf16[48,1024]{1,0:T(8,128)(2,1)S(1)} %maximum_select_fusion.refs_0_), channel_id=1, source_target_pairs={{0,64},{64,128},{128,192},{192,0},{1,65},{65,129},{129,193},{193,1... | collective-permute-start | bytes 294920 | tf_op jit(solution)/shard_map/ppermute | solution.py:288
  6.5 6.6 %collective-permute-start.2 = (bf16[48,1024]{1,0:T(8,128)(2,1)S(1)}, bf16[48,1024]{1,0:T(8,128)(2,1)S(1)}, u32[]{:S(2)}, u32[]{:S(2)}) collective-permute-start(bf16[48,1024]{1,0:T(8,128)(2,1)S(1)} %maximum_select_fusion.refs_0_), channel_id=1, source_target_pairs={{0,128},{64,192},{128,0},{192,64},{1,129},{65,193},{129,1},{193,65... | collective-permute-start | bytes 294920 | tf_op jit(solution)/shard_map/ppermute | solution.py:288
  8.4 5.7 %collective-permute-start.3 = (bf16[48,1024]{1,0:T(8,128)(2,1)S(1)}, bf16[48,1024]{1,0:T(8,128)(2,1)S(1)}, u32[]{:S(2)}, u32[]{:S(2)}) collective-permute-start(bf16[48,1024]{1,0:T(8,128)(2,1)S(1)} %maximum_select_fusion.refs_0_), channel_id=1, source_target_pairs={{0,192},{64,0},{128,64},{192,128},{1,193},{65,1},{129,65},{193,129... | collective-permute-start | bytes 294920 | tf_op jit(solution)/shard_map/ppermute | solution.py:288
  15.0 16.7 %collective-permute-start.4 = (bf16[48,4096]{1,0:T(8,128)(2,1)S(1)}, bf16[48,4096]{1,0:T(8,128)(2,1)S(1)}, u32[]{:S(2)}, u32[]{:S(2)}) collective-permute-start(bf16[48,4096]{1,0:T(8,128)(2,1)S(1)} %shard_map.66.refs_0_), channel_id=1, source_target_pairs={{0,4},{4,8},{8,12},{12,16},{16,20},{20,24},{24,28},{28,0},{1,5},{5... | collective-permute-start | bytes 1179656 | tf_op jit(solution)/shard_map/ppermute | solution.py:299
  15.6 16.1 %collective-permute-start.8 = (bf16[48,4096]{1,0:T(8,128)(2,1)S(1)}, bf16[48,4096]{1,0:T(8,128)(2,1)S(1)}, u32[]{:S(2)}, u32[]{:S(2)}) collective-permute-start(bf16[48,4096]{1,0:T(8,128)(2,1)S(1)} %shard_map.66.refs_0_), channel_id=1, source_target_pairs={{0,28},{4,0},{8,4},{12,8},{16,12},{20,16},{24,20},{28,24},{1,29},{... | collective-permute-start | bytes 1179656 | tf_op jit(solution)/shard_map/ppermute | solution.py:299
  31.7 26.7 %collective-permute-start.5 = (bf16[48,4096]{1,0:T(8,128)(2,1)S(1)}, bf16[48,4096]{1,0:T(8,128)(2,1)S(1)}, u32[]{:S(2)}, u32[]{:S(2)}) collective-permute-start(bf16[48,4096]{1,0:T(8,128)(2,1)S(1)} %collective-permute-done.4.refs_0_), channel_id=1, source_target_pairs={{0,4},{4,8},{8,12},{12,16},{16,20},{20,24},{24,28},{28,0},{1,5},{5... | collective-permute-start | bytes 1179656 | tf_op jit(solution)/shard_map/ppermute | solution.py:302
  31.8 26.7 %collective-permute-start.9 = (bf16[48,4096]{1,0:T(8,128)(2,1)S(1)}, bf16[48,4096]{1,0:T(8,128)(2,1)S(1)}, u32[]{:S(2)}, u32[]{:S(2)}) collective-permute-start(bf16[48,4096]{1,0:T(8,128)(2,1)S(1)} %collective-permute-done.8.refs_1_), channel_id=1, source_target_pairs={{0,28},{4,0},{8,4},{12,8},{16,12},{20,16},{24,20},{28,24},{1,29},{... | collective-permute-start | bytes 1179656 | tf_op jit(solution)/shard_map/ppermute | solution.py:303
  58.4 26.7 %collective-permute-start.6 = (bf16[48,4096]{1,0:T(8,128)(2,1)S(1)}, bf16[48,4096]{1,0:T(8,128)(2,1)S(1)}, u32[]{:S(2)}, u32[]{:S(2)}) collective-permute-start(bf16[48,4096]{1,0:T(8,128)(2,1)S(1)} %collective-permute-done.5.refs_0_), channel_id=1, source_target_pairs={{0,4},{4,8},{8,12},{12,16},{16,20},{20,24},{24,28},{28,0},{1,5},{5... | collective-permute-start | bytes 1179656 | tf_op jit(solution)/shard_map/ppermute | solution.py:302
  58.5 26.9 %collective-permute-start.10 = (bf16[48,4096]{1,0:T(8,128)(2,1)S(1)}, bf16[48,4096]{1,0:T(8,128)(2,1)S(1)}, u32[]{:S(2)}, u32[]{:S(2)}) collective-permute-start(bf16[48,4096]{1,0:T(8,128)(2,1)S(1)} %collective-permute-done.9.refs_1_), channel_id=1, source_target_pairs={{0,28},{4,0},{8,4},{12,8},{16,12},{20,16},{24,20},{28,24},{1,29},{... | collective-permute-start | bytes 1179656 | tf_op jit(solution)/shard_map/ppermute | solution.py:303
  85.1 24.3 %collective-permute-start.7 = (bf16[48,4096]{1,0:T(8,128)(2,1)S(1)}, bf16[48,4096]{1,0:T(8,128)(2,1)S(1)}, u32[]{:S(2)}, u32[]{:S(2)}) collective-permute-start(bf16[48,4096]{1,0:T(8,128)(2,1)S(1)} %collective-permute-done.6.refs_0_), channel_id=1, source_target_pairs={{0,4},{4,8},{8,12},{12,16},{16,20},{20,24},{24,28},{28,0},{1,5},{5... | collective-permute-start | bytes 1179656 | tf_op jit(solution)/shard_map/ppermute | solution.py:302
  122.0 5.0 %collective-permute-start.11 = (f32[40,512]{1,0:T(8,128)S(1)}, f32[40,512]{1,0:T(8,128)S(1)}, u32[]{:S(2)}, u32[]{:S(2)}) collective-permute-start(f32[40,512]{1,0:T(8,128)S(1)} %get-tuple-element.32), channel_id=1, source_target_pairs={{0,1},{1,2},{2,3},{3,0},{4,5},{5,6},{6,7},{7,4},{8,9},{9,10},{10,1... | collective-permute-start | bytes 245768 | tf_op jit(solution)/shard_map/ppermute | solution.py:308
  123.3 5.3 %collective-permute-start.12 = (f32[40,512]{1,0:T(8,128)S(1)}, f32[40,512]{1,0:T(8,128)S(1)}, u32[]{:S(2)}, u32[]{:S(2)}) collective-permute-start(f32[40,512]{1,0:T(8,128)S(1)} %get-tuple-element.33), channel_id=1, source_target_pairs={{0,2},{1,3},{2,0},{3,1},{4,6},{5,7},{6,4},{7,5},{8,10},{9,11},{10,... | collective-permute-start | bytes 245768 | tf_op jit(solution)/shard_map/ppermute | solution.py:308
  125.9 3.6 %collective-permute-start.13 = (f32[40,512]{1,0:T(8,128)S(1)}, f32[40,512]{1,0:T(8,128)S(1)}, u32[]{:S(2)}, u32[]{:S(2)}) collective-permute-start(f32[40,512]{1,0:T(8,128)S(1)} %get-tuple-element.34), channel_id=1, source_target_pairs={{0,3},{1,0},{2,1},{3,2},{4,7},{5,4},{6,5},{7,6},{8,11},{9,8},{10,9... | collective-permute-start | bytes 245768 | tf_op jit(solution)/shard_map/ppermute | solution.py:308
where the time goes:
time: 164 us
  Pallas kernels  102 us (62%)
  blocking collectives  30.1 us (18%)
  starting transfers between devices  21.9 us (13%)
  waiting for transfers between devices  7.94 us (5%)
    pallas_call x5, Pallas kernels, partial_drive(): pl.pallas_call(functools.partial(drive_kernel, shifts=shifts, earlier=len...  96.4 us
    all_to_all x1, blocking collectives, gather_grams(): near = jnp.sum(lax.all_to_all(copies, ('x', 'core', 'y'), 0, 0), axis=0)  17.4 us
    all_to_all x1, blocking collectives, gather_grams(): return lax.all_to_all(jnp.broadcast_to(near, (Z, *near.shape)), 'z', 0, 0)  12.7 us
    ppermute x2, starting transfers between devices, per_device(): next_above = lax.ppermute(above, 'z', down) if step + 1 < Z // 2 else None  5.31 us
    ppermute x3, starting transfers between devices, per_device(): lax.ppermute(pieces[shift], 'y', [(i, (i + shift) % Y) for i in range(Y)])  4.98 us
    ppermute x2, starting transfers between devices, per_device(): below, above = (lax.ppermute(near, 'z', up), lax.ppermute(near, 'z', down))  4.69 us
    ppermute x3, waiting for transfers between devices, per_device(): lax.ppermute(pair, 'x', [(i, (i + shift) % X) for i in range(X)])  4.53 us
    ppermute x1, starting transfers between devices, per_device(): other = lax.ppermute(own, 'core', [(0, 1), (1, 0)])  3.33 us
  transfers between devices with their start and end apart: 14, of which 6 were waited for; matrix products, arithmetic and copies ran while one was open for 0% of the time, Pallas kernels for 51%

commit v1 on v0

--- a/solution.py
+++ b/solution.py
@@ -49,12 +49,22 @@
     return block_ref[SPARE - 8 : SPARE + 8, 128 * tile : 128 * tile + 128].astype(jnp.float32)[8:]
 
 
-def block_kernel(keys_ref, *refs):
-    pair_refs, block_ref = refs[:X], refs[X]
-    wide = CORE * OWN
-    for shift in range(X):
-        chip = lax.rem(lax.axis_index("x") + X - shift, X)
-        block_ref[:, pl.ds(pl.multiple_of(chip * wide, wide), wide)] = pair_refs[shift][...]
+def own_kernel(tangent_ref, activity_ref, own_ref):
+    parts = [activity_ref[k : k + 1, :].astype(jnp.float32) for k in range(OWN // 128)]
+    rest = jnp.zeros((PAD - VECS - 1, OWN), jnp.float32)
+    rest = jnp.concatenate((jnp.concatenate(parts, axis=1), rest))
+    own_ref[:VECS, :] = tangent_ref[...]
+    own_ref[VECS:, :] = rest.astype(jnp.bfloat16)
+
+
+def block_kernel(keys_ref, mine_ref, others_ref, block_ref):
+    shards_refs = (mine_ref, others_ref)
+    for core in range(CORE):
+        at = jnp.bitwise_xor(lax.axis_index("core"), core) * OWN
+        for shift in range(X):
+            chip = lax.rem(lax.axis_index("x") + (X - shift), X)
+            lanes = pl.ds(pl.multiple_of(chip * (CORE * OWN) + at, OWN), OWN)
+            block_ref[:, lanes] = shards_refs[core][shift]
     own = block_ref[:VECS, :]
     gram = lax.dot_general(own, own, (((1,), (1,)), ((), ())), preferred_element_type=jnp.float32)
     rest = pack_gram(gram / N)
@@ -79,7 +89,7 @@
         block_ref[SPARE - 8 : SPARE + 8, lanes] = jnp.concatenate((above, tile)).astype(jnp.bfloat16)
 
 
-def drive_kernel(*refs, shifts, earlier, last):
+def drive_kernel(*refs, shifts, earlier, parts):
     blocks = len(shifts)
     block_refs = refs[:blocks]
     earlier_refs = refs[blocks : blocks + 2 * earlier]
@@ -108,12 +118,15 @@
                 at = k * groups + key * 8
                 bases_ref[at : at + 8, :] = keys[row : row + 1] + columns * jnp.int32(668265261)
 
+    def part_at(number):
+        return lax.rem(lax.axis_index("y") + (parts[0] + number), Y) if parts else number
+
     first_row = (lax.axis_index("x") * CORE + lax.axis_index("core")) * (N // (X * CORE)) + lax.axis_index("z") * ROWS
     row_at = lax.broadcasted_iota(jnp.int32, (GROUP, 128), 1)
     spread = lax.broadcasted_iota(jnp.int32, (GROUP, 128), 0) * jnp.int32(668265261)
 
-    def lanes_body(part, carry):
-        lane = pl.multiple_of(part * LANES, LANES)
+    def lanes_body(number, carry):
+        lane = pl.multiple_of(part_at(number) * LANES, LANES)
         starts = [
             (first_row + lane + 128 * k + row_at) * jnp.int32(374761393) + spread
             for k in range(LANES // 128)
@@ -136,30 +149,30 @@
         total_ref[:, here] = lax.fori_loop(0, blocks, body, initial)
         return carry
 
-    lax.fori_loop(0, ROWS // LANES, lanes_body, 0)
-    if not last:
+    lax.fori_loop(0, len(parts) or Y, lanes_body, 0)
+    if not parts:
         out_refs[0][...] = total_ref[...]
         return
     gram = grams_ref[0]
     for slot in range(1, Z):
         gram = gram + grams_ref[slot]
-    for shift, out_ref in enumerate(out_refs):
-        to = lax.rem(lax.axis_index("y") + shift, Y)
-        out_ref[...] = total_ref[:SENT, pl.ds(pl.multiple_of(to * OWN, OWN), OWN)]
+    for number, out_ref in enumerate(out_refs):
+        lane = pl.multiple_of(part_at(number) * LANES, LANES)
+        out_ref[...] = total_ref[:SENT, pl.ds(lane, LANES)]
         out_ref[GRAM_ROW:, :128] = gram[:4]
         out_ref[GRAM_ROW:, 128:256] = gram[4:]
 
 
-def partial_drive(shifts, blocks, earlier=(), last=False):
+def partial_drive(shifts, blocks, earlier=(), parts=()):
     count = len(blocks)
     drive = jax.ShapeDtypeStruct((PAD, ROWS), jnp.float32)
-    if last:
-        out_shape = [jax.ShapeDtypeStruct((SENT, OWN), jnp.float32)] * Y
+    if parts:
+        out_shape = [jax.ShapeDtypeStruct((SENT, OWN), jnp.float32)] * len(parts)
     else:
         out_shape = [drive]
     grams = jax.ShapeDtypeStruct((Z, 8, 128), jnp.float32)
     return pl.pallas_call(
-        functools.partial(drive_kernel, shifts=shifts, earlier=len(earlier) // 2, last=last),
+        functools.partial(drive_kernel, shifts=shifts, earlier=len(earlier) // 2, parts=parts),
         in_specs=[VMEM] * (count + len(earlier)),
         out_specs=[VMEM] * (len(out_shape) + 1),
         out_shape=out_shape + [grams],
@@ -169,7 +182,9 @@
             pltpu.VMEM((count * SEG // GROUP, 128), jnp.int32),
         ],
         cost_estimate=pl.CostEstimate(
-            flops=count * SEG * ROWS * 1500, bytes_accessed=count * PAD * SEG * 2, transcendentals=0
+            flops=count * SEG * (len(parts) or Y) * LANES * 1500,
+            bytes_accessed=count * PAD * SEG * 2,
+            transcendentals=0,
         ),
         compiler_params=PARAMS,
     )(*blocks, *earlier)
@@ -275,24 +290,24 @@
 
 
 def per_device(tangent, activity, block_keys):
-    own = jnp.concatenate(
-        (tangent, activity.reshape(1, -1), jnp.zeros((PAD - VECS - 1, OWN), jnp.bfloat16)), axis=0
+    block = jax.ShapeDtypeStruct((PAD, OWN), jnp.bfloat16)
+    own = pl.pallas_call(own_kernel, out_shape=block, compiler_params=PARAMS)(
+        tangent, activity.reshape(OWN // 128, 128)
     )
-    other = lax.ppermute(own, "core", [(0, 1), (1, 0)])
-    pair = jnp.where(
-        lax.axis_index("core") == 0,
-        jnp.concatenate((own, other), axis=1),
-        jnp.concatenate((other, own), axis=1),
+    mine = jnp.stack(
+        [own]
+        + [
+            lax.ppermute(own, "x", [(i, (i + shift) % X) for i in range(X)])
+            for shift in range(1, X)
+        ]
     )
-    pairs = [pair] + [
-        lax.ppermute(pair, "x", [(i, (i + shift) % X) for i in range(X)]) for shift in range(1, X)
-    ]
+    others = lax.ppermute(mine, "core", [(0, 1), (1, 0)])
     near = pl.pallas_call(
         block_kernel,
-        in_specs=[SMEM] + [VMEM] * X,
+        in_specs=[SMEM, VMEM, VMEM],
         out_shape=jax.ShapeDtypeStruct((PAD, SEG), jnp.bfloat16),
         compiler_params=PARAMS,
-    )(block_keys, *pairs)
+    )(block_keys, mine, others)
 
     up = [(i, (i + 1) % Z) for i in range(Z)]
     down = [(i, (i - 1) % Z) for i in range(Z)]
@@ -303,9 +318,12 @@
         next_above = lax.ppermute(above, "z", down) if step + 1 < Z // 2 else None
         earlier = partial_drive((-step, step), [below, above], earlier)
         below, above = next_below, next_above
-    *pieces, _ = partial_drive((Z // 2,), [below], earlier, last=True)
-    for shift in range(1, Y):
-        pieces[shift] = lax.ppermute(pieces[shift], "y", [(i, (i + shift) % Y) for i in range(Y)])
+    *sent, _ = partial_drive((Z // 2,), [below], earlier, tuple(range(1, Y)))
+    kept, _ = partial_drive((Z // 2,), [below], earlier, (0,))
+    pieces = [kept] + [
+        lax.ppermute(piece, "y", [(i, (i + shift) % Y) for i in range(Y)])
+        for shift, piece in enumerate(sent, 1)
+    ]
 
     square = jax.ShapeDtypeStruct((VECS, VECS), jnp.float32)
     wide = jax.ShapeDtypeStruct((VECS, OWN), jnp.float32)

time: 164 us -> 161 us (0.982)
  waiting for transfers between devices: 7.94 us -> 3.18 us
  starting transfers between devices: 21.9 us -> 24.4 us
  blocking collectives: 30.1 us -> 28.2 us
    ppermute x7, waiting for transfers between devices: 7.92 us -> 3.16 us  [the longest x3 2.08 us: per_device(): lax.ppermute(own, 'x', [(i, (i + shift) % X) for i in range(X)])]
    all_to_all x1, blocking collectives: 17.4 us -> 15.5 us  [gather_grams(): near = jnp.sum(lax.all_to_all(copies, ('x', 'core', 'y'), 0, 0), axis=0)]
    pallas_call x5 -> x6, Pallas kernels: 96.4 us -> 97 us  [partial_drive(): pl.pallas_call(functools.partial(drive_kernel, shifts=shifts, earlier=len...]
  transfers between devices with their start and end apart: 14 -> 14, of which waited for: 6 -> 3; matrix products, arithmetic and copies ran while one was open for 0% -> 0% of each run, Pallas kernels for 51% -> 54%
where the time goes in v1:
time: 161 us; the launch traced here: 160 us
  Pallas kernels  102 us (63%)
  blocking collectives  28.2 us (18%)
  starting transfers between devices  24.4 us (15%)
  waiting for transfers between devices  3.18 us (2%)
    pallas_call x6, Pallas kernels, partial_drive(): pl.pallas_call(functools.partial(drive_kernel, shifts=shifts, earlier=len...  97 us
    all_to_all x1, blocking collectives, gather_grams(): near = jnp.sum(lax.all_to_all(copies, ('x', 'core', 'y'), 0, 0), axis=0)  15.5 us
    all_to_all x1, blocking collectives, gather_grams(): return lax.all_to_all(jnp.broadcast_to(near, (Z, *near.shape)), 'z', 0, 0)  12.7 us
    ppermute x3, starting transfers between devices, per_device(): lax.ppermute(own, 'x', [(i, (i + shift) % X) for i in range(X)])  5.72 us
    ppermute x2, starting transfers between devices, per_device(): below, above = (lax.ppermute(near, 'z', up), lax.ppermute(near, 'z', down))  5.58 us
    ppermute x2, starting transfers between devices, per_device(): next_above = lax.ppermute(above, 'z', down) if step + 1 < Z // 2 else None  5.31 us
    ppermute x3, starting transfers between devices, per_device(): lax.ppermute(piece, 'y', [(i, (i + shift) % Y) for i in range(Y)])  4.99 us
  transfers between devices with their start and end apart: 14, of which 3 were waited for; matrix products, arithmetic and copies ran while one was open for 0% of the time, Pallas kernels for 54%

profile of v1, /device:TPU:1, one launch (start us, length us, event | category | flops | bytes accessed | tf_op | source)
XLA Modules:
  0.0 160.5 jit_solution(1060395851250119228)
XLA Ops:
  2.1 2.1 %collective-permute-start = (bf16[48,512]{1,0:T(8,128)(2,1)S(1)}, bf16[48,512]{1,0:T(8,128)(2,1)S(1)}, u32[]{:S(2)}, u32[]{:S(2)}) collective-permute-start(bf16[48,512]{1,0:T(8,128)(2,1)S(1)} %shard_map.66), channel_id=1, source_target_pairs={{0,64},{64,128},{128,192},{192,0},{1,65},{65,129},{129,193},{193,1... | collective-permute-start | bytes 147464 | tf_op jit(solution)/shard_map/ppermute | solution.py:300
  4.2 2.5 %collective-permute-start.1 = (bf16[48,512]{1,0:T(8,128)(2,1)S(1)}, bf16[48,512]{1,0:T(8,128)(2,1)S(1)}, u32[]{:S(2)}, u32[]{:S(2)}) collective-permute-start(bf16[48,512]{1,0:T(8,128)(2,1)S(1)} %shard_map.66), channel_id=1, source_target_pairs={{0,128},{64,192},{128,0},{192,64},{1,129},{65,193},{129,1},{193,65... | collective-permute-start | bytes 147464 | tf_op jit(solution)/shard_map/ppermute | solution.py:300
  6.6 1.2 collective-permute-start.2
  8.7 1.2 collective-permute-done.2
  9.9 2.3 %collective-permute-start.3 = (bf16[4,48,512]{2,1,0:T(8,128)(2,1)S(1)}, bf16[4,48,512]{2,1,0:T(8,128)(2,1)S(1)}, u32[]{:S(2)}, u32[]{:S(2)}) collective-permute-start(bf16[4,48,512]{2,1,0:T(8,128)(2,1)S(1)} %pad_maximum_fusion.mine_ref), channel_id=1, source_target_pairs={{0,32},{32,0},{1,33},{33,1},{2,34},{34,2},{3,35},{35,3},{4,36},{36... | collective-permute-start | bytes 589832 | tf_op jit(solution)/shard_map/ppermute | solution.py:304
  12.2 1.1 collective-permute-done.3.others_ref
  13.3 0.9 shard_map.67.refs_0_
  14.1 1.6 collective-permute-start.4
  15.7 4.0 %collective-permute-start.8 = (bf16[48,4096]{1,0:T(8,128)(2,1)S(1)}, bf16[48,4096]{1,0:T(8,128)(2,1)S(1)}, u32[]{:S(2)}, u32[]{:S(2)}) collective-permute-start(bf16[48,4096]{1,0:T(8,128)(2,1)S(1)} %shard_map.67.refs_0_), channel_id=1, source_target_pairs={{0,28},{4,0},{8,4},{12,8},{16,12},{20,16},{24,20},{28,24},{1,29},{... | collective-permute-start | bytes 1179656 | tf_op jit(solution)/shard_map/ppermute | solution.py:314
  19.7 12.0 %shard_map.68 = (f32[48,2048]{1,0:T(8,128)S(1)}, f32[8,8,128]{2,1,0:T(8,128)S(1)}) custom-call(bf16[48,4096]{1,0:T(8,128)(2,1)S(1)} %shard_map.67.refs_0_), custom_call_target="tpu_custom_call" | custom-call | flops 12582912000 | bytes 393216 | tf_op jit(solution)/shard_map/pallas_call | solution.py:174
  31.8 2.7 %collective-permute-start.9 = (bf16[48,4096]{1,0:T(8,128)(2,1)S(1)}, bf16[48,4096]{1,0:T(8,128)(2,1)S(1)}, u32[]{:S(2)}, u32[]{:S(2)}) collective-permute-start(bf16[48,4096]{1,0:T(8,128)(2,1)S(1)} %collective-permute-done.8.refs_1_), channel_id=1, source_target_pairs={{0,28},{4,0},{8,4},{12,8},{16,12},{20,16},{24,20},{28,24},{1,29},{... | collective-permute-start | bytes 1179656 | tf_op jit(solution)/shard_map/ppermute | solution.py:318
  34.5 24.0 %shard_map.69 = (f32[48,2048]{1,0:T(8,128)S(1)}, f32[8,8,128]{2,1,0:T(8,128)S(1)}) custom-call(bf16[48,4096]{1,0:T(8,128)(2,1)S(1)} %collective-permute-done.4.refs_0_, bf16[48,4096]{1,0:T(8,128)(2,1)S(1)} %collective-permute-done.8.refs_1_, f32[48,2048]{1,0:T(8,128)S(1)} %get-tuple-element.23.refs_2_, f32[8,8,128]{2,1,0:T(8,128)S(1)} %get-tuple-element.24.refs_3_), custom_call_target="tpu_custom_call" | custom-call | flops 25165824000 | bytes 786432 | tf_op jit(solution)/shard_map/pallas_call | solution.py:174
  58.6 2.7 %collective-permute-start.10 = (bf16[48,4096]{1,0:T(8,128)(2,1)S(1)}, bf16[48,4096]{1,0:T(8,128)(2,1)S(1)}, u32[]{:S(2)}, u32[]{:S(2)}) collective-permute-start(bf16[48,4096]{1,0:T(8,128)(2,1)S(1)} %collective-permute-done.9.refs_1_), channel_id=1, source_target_pairs={{0,28},{4,0},{8,4},{12,8},{16,12},{20,16},{24,20},{28,24},{1,29},{... | collective-permute-start | bytes 1179656 | tf_op jit(solution)/shard_map/ppermute | solution.py:318
  61.2 24.0 %shard_map.70 = (f32[48,2048]{1,0:T(8,128)S(1)}, f32[8,8,128]{2,1,0:T(8,128)S(1)}) custom-call(bf16[48,4096]{1,0:T(8,128)(2,1)S(1)} %collective-permute-done.5.refs_0_, bf16[48,4096]{1,0:T(8,128)(2,1)S(1)} %collective-permute-done.9.refs_1_, f32[48,2048]{1,0:T(8,128)S(1)} %get-tuple-element.25.refs_2_, f32[8,8,128]{2,1,0:T(8,128)S(1)} %get-tuple-element.26.refs_3_), custom_call_target="tpu_custom_call" | custom-call | flops 25165824000 | bytes 786432 | tf_op jit(solution)/shard_map/pallas_call | solution.py:174
  85.5 24.0 %shard_map.71 = (f32[48,2048]{1,0:T(8,128)S(1)}, f32[8,8,128]{2,1,0:T(8,128)S(1)}) custom-call(bf16[48,4096]{1,0:T(8,128)(2,1)S(1)} %collective-permute-done.6.refs_0_, bf16[48,4096]{1,0:T(8,128)(2,1)S(1)} %collective-permute-done.10.refs_1_, f32[48,2048]{1,0:T(8,128)S(1)} %get-tuple-element.27.refs_2_, f32[8,8,128]{2,1,0:T(8,128)S(1)} %get-tuple-element.28.refs_3_), custom_call_target="tpu_custom_call" | custom-call | flops 25165824000 | bytes 786432 | tf_op jit(solution)/shard_map/pallas_call | solution.py:174
  109.5 9.6 %shard_map.73 = (f32[40,512]{1,0:T(8,128)S(1)}, f32[40,512]{1,0:T(8,128)S(1)}, f32[40,512]{1,0:T(8,128)S(1)}, f32[8,8,128]{2,1,0:T(8,128)}) custom-call(bf16[48,4096]{1,0:T(8,128)(2,1)S(1)} %collective-permute-done.7.refs_0_, f32[48,2048]{1,0:T(8,128)S(1)} %get-tuple-element.29.refs_1_, f32[8,8,128]{2,1,0:T(8,128)S(1)} %get-tuple-element.30.refs_2_), custom_call_target="tpu_custom_call" | custom-call | flops 9437184000 | bytes 393216 | tf_op jit(solution)/shard_map/pallas_call | solution.py:174
  119.1 1.3 collective-permute-start.11
  120.4 2.6 %collective-permute-start.12 = (f32[40,512]{1,0:T(8,128)S(1)}, f32[40,512]{1,0:T(8,128)S(1)}, u32[]{:S(2)}, u32[]{:S(2)}) collective-permute-start(f32[40,512]{1,0:T(8,128)S(1)} %get-tuple-element.33), channel_id=1, source_target_pairs={{0,2},{1,3},{2,0},{3,1},{4,6},{5,7},{6,4},{7,5},{8,10},{9,11},{10,... | collective-permute-start | bytes 245768 | tf_op jit(solution)/shard_map/ppermute | solution.py:324
  123.0 1.1 collective-permute-start.13
  124.1 3.6 %shard_map.72 = (f32[40,512]{1,0:T(8,128)S(1)}, f32[8,8,128]{2,1,0:T(8,128)}) custom-call(bf16[48,4096]{1,0:T(8,128)(2,1)S(1)} %collective-permute-done.7.refs_0_, f32[48,2048]{1,0:T(8,128)S(1)} %get-tuple-element.29.refs_1_, f32[8,8,128]{2,1,0:T(8,128)S(1)} %get-tuple-element.30.refs_2_), custom_call_target="tpu_custom_call" | custom-call | flops 3145728000 | bytes 393216 | tf_op jit(solution)/shard_map/pallas_call | solution.py:174
  127.7 1.8 %shard_map.74 = (f32[1,512]{1,0:T(1,128)}, f32[32,512]{1,0:T(8,128)S(1)}, f32[32,8,128]{2,1,0:T(8,128)S(1)}, f32[32,32]{1,0:T(8,128)S(1)}) custom-call(f32[40,512]{1,0:T(8,128)S(1)} %get-tuple-element.31.mine_ref, f32[40,512]{1,0:T(8,128)S(1)} %collective-permute-done.11.others_ref, f32[40,512]{1,0:T(8,128)S(1)} %collective-permute-done.12.refs_0_, ...), custom_call_target="tpu_custom_call" | custom-call | tf_op jit(solution)/shard_map/pallas_call | solution.py:330
  129.5 15.5 %all_to_all.10 = f32[32,8,128]{2,1,0:T(8,128)S(1)} all-to-all(f32[32,8,128]{2,1,0:T(8,128)S(1)} %get-tuple-element.35), channel_id=1, replica_groups=mesh['x'=4,'core'=2,'z'=8,'y'=4] {'x','core','y'}, dimensions={0} | all-to-all | bytes 262144 | tf_op jit(solution)/shard_map/all_to_all | solution.py:288
  145.1 12.7 %all_to_all.11.grams_ref = f32[8,8,128]{2,1,0:T(8,128)S(1)} all-to-all(f32[8,8,128]{2,1,0:T(8,128)S(1)} %broadcast_in_dim.3), channel_id=1, replica_groups=mesh['x'=4,'core'=2,'z'=8,'y'=4] {'z'}, dimensions={0} | all-to-all | bytes 65536 | tf_op jit(solution)/shard_map/all_to_all | solution.py:289
  157.8 2.7 %shard_map.75 = (f32[32,512]{1,0:T(8,128)}, f32[32,32]{1,0:T(8,128)}, f32[32,32]{1,0:T(8,128)}) custom-call(f32[8,8,128]{2,1,0:T(8,128)S(1)} %all_to_all.11.grams_ref, f32[32,512]{1,0:T(8,128)S(1)} %get-tuple-element.36.scaled_ref, f32[32,32]{1,0:T(8,128)S(1)} %get-tuple-element.37.input_upper_ref), custom_call_target="tpu_custom_call" | custom-call | tf_op jit(solution)/shard_map/pallas_call | solution.py:341
  (25 shorter events, 2.9 us)
Async XLA Ops:
  0.6 0.7 copy-start.1
  1.3 0.8 copy-start
  2.1 5.7 %collective-permute-start = (bf16[48,512]{1,0:T(8,128)(2,1)S(1)}, bf16[48,512]{1,0:T(8,128)(2,1)S(1)}, u32[]{:S(2)}, u32[]{:S(2)}) collective-permute-start(bf16[48,512]{1,0:T(8,128)(2,1)S(1)} %shard_map.66), channel_id=1, source_target_pairs={{0,64},{64,128},{128,192},{192,0},{1,65},{65,129},{129,193},{193,1... | collective-permute-start | bytes 147464 | tf_op jit(solution)/shard_map/ppermute | solution.py:300
  4.2 4.5 %collective-permute-start.1 = (bf16[48,512]{1,0:T(8,128)(2,1)S(1)}, bf16[48,512]{1,0:T(8,128)(2,1)S(1)}, u32[]{:S(2)}, u32[]{:S(2)}) collective-permute-start(bf16[48,512]{1,0:T(8,128)(2,1)S(1)} %shard_map.66), channel_id=1, source_target_pairs={{0,128},{64,192},{128,0},{192,64},{1,129},{65,193},{129,1},{193,65... | collective-permute-start | bytes 147464 | tf_op jit(solution)/shard_map/ppermute | solution.py:300
  6.6 3.2 %collective-permute-start.2 = (bf16[48,512]{1,0:T(8,128)(2,1)S(1)}, bf16[48,512]{1,0:T(8,128)(2,1)S(1)}, u32[]{:S(2)}, u32[]{:S(2)}) collective-permute-start(bf16[48,512]{1,0:T(8,128)(2,1)S(1)} %shard_map.66), channel_id=1, source_target_pairs={{0,192},{64,0},{128,64},{192,128},{1,193},{65,1},{129,65},{193,129... | collective-permute-start | bytes 147464 | tf_op jit(solution)/shard_map/ppermute | solution.py:300
  9.9 3.4 %copy-start.2 = (s32[1,16]{1,0:T(1,128)S(1)}, s32[1,16]{1,0:T(1,128)}, u32[]{:S(2)}) copy-start(s32[1,16]{1,0:T(1,128)} %keys_ref.1) | copy-start | bytes 196
  9.9 3.4 %collective-permute-start.3 = (bf16[4,48,512]{2,1,0:T(8,128)(2,1)S(1)}, bf16[4,48,512]{2,1,0:T(8,128)(2,1)S(1)}, u32[]{:S(2)}, u32[]{:S(2)}) collective-permute-start(bf16[4,48,512]{2,1,0:T(8,128)(2,1)S(1)} %pad_maximum_fusion.mine_ref), channel_id=1, source_target_pairs={{0,32},{32,0},{1,33},{33,1},{2,34},{34,2},{3,35},{35,3},{4,36},{36... | collective-permute-start | bytes 589832 | tf_op jit(solution)/shard_map/ppermute | solution.py:304
  14.1 17.6 %collective-permute-start.4 = (bf16[48,4096]{1,0:T(8,128)(2,1)S(1)}, bf16[48,4096]{1,0:T(8,128)(2,1)S(1)}, u32[]{:S(2)}, u32[]{:S(2)}) collective-permute-start(bf16[48,4096]{1,0:T(8,128)(2,1)S(1)} %shard_map.67.refs_0_), channel_id=1, source_target_pairs={{0,4},{4,8},{8,12},{12,16},{16,20},{20,24},{24,28},{28,0},{1,5},{5... | collective-permute-start | bytes 1179656 | tf_op jit(solution)/shard_map/ppermute | solution.py:314
  15.7 16.1 %collective-permute-start.8 = (bf16[48,4096]{1,0:T(8,128)(2,1)S(1)}, bf16[48,4096]{1,0:T(8,128)(2,1)S(1)}, u32[]{:S(2)}, u32[]{:S(2)}) collective-permute-start(bf16[48,4096]{1,0:T(8,128)(2,1)S(1)} %shard_map.67.refs_0_), channel_id=1, source_target_pairs={{0,28},{4,0},{8,4},{12,8},{16,12},{20,16},{24,20},{28,24},{1,29},{... | collective-permute-start | bytes 1179656 | tf_op jit(solution)/shard_map/ppermute | solution.py:314
  31.7 26.7 %collective-permute-start.5 = (bf16[48,4096]{1,0:T(8,128)(2,1)S(1)}, bf16[48,4096]{1,0:T(8,128)(2,1)S(1)}, u32[]{:S(2)}, u32[]{:S(2)}) collective-permute-start(bf16[48,4096]{1,0:T(8,128)(2,1)S(1)} %collective-permute-done.4.refs_0_), channel_id=1, source_target_pairs={{0,4},{4,8},{8,12},{12,16},{16,20},{20,24},{24,28},{28,0},{1,5},{5... | collective-permute-start | bytes 1179656 | tf_op jit(solution)/shard_map/ppermute | solution.py:317
  31.8 26.7 %collective-permute-start.9 = (bf16[48,4096]{1,0:T(8,128)(2,1)S(1)}, bf16[48,4096]{1,0:T(8,128)(2,1)S(1)}, u32[]{:S(2)}, u32[]{:S(2)}) collective-permute-start(bf16[48,4096]{1,0:T(8,128)(2,1)S(1)} %collective-permute-done.8.refs_1_), channel_id=1, source_target_pairs={{0,28},{4,0},{8,4},{12,8},{16,12},{20,16},{24,20},{28,24},{1,29},{... | collective-permute-start | bytes 1179656 | tf_op jit(solution)/shard_map/ppermute | solution.py:318
  58.5 26.7 %collective-permute-start.6 = (bf16[48,4096]{1,0:T(8,128)(2,1)S(1)}, bf16[48,4096]{1,0:T(8,128)(2,1)S(1)}, u32[]{:S(2)}, u32[]{:S(2)}) collective-permute-start(bf16[48,4096]{1,0:T(8,128)(2,1)S(1)} %collective-permute-done.5.refs_0_), channel_id=1, source_target_pairs={{0,4},{4,8},{8,12},{12,16},{16,20},{20,24},{24,28},{28,0},{1,5},{5... | collective-permute-start | bytes 1179656 | tf_op jit(solution)/shard_map/ppermute | solution.py:317
  58.6 26.9 %collective-permute-start.10 = (bf16[48,4096]{1,0:T(8,128)(2,1)S(1)}, bf16[48,4096]{1,0:T(8,128)(2,1)S(1)}, u32[]{:S(2)}, u32[]{:S(2)}) collective-permute-start(bf16[48,4096]{1,0:T(8,128)(2,1)S(1)} %collective-permute-done.9.refs_1_), channel_id=1, source_target_pairs={{0,28},{4,0},{8,4},{12,8},{16,12},{20,16},{24,20},{28,24},{1,29},{... | collective-permute-start | bytes 1179656 | tf_op jit(solution)/shard_map/ppermute | solution.py:318
  85.2 24.3 %collective-permute-start.7 = (bf16[48,4096]{1,0:T(8,128)(2,1)S(1)}, bf16[48,4096]{1,0:T(8,128)(2,1)S(1)}, u32[]{:S(2)}, u32[]{:S(2)}) collective-permute-start(bf16[48,4096]{1,0:T(8,128)(2,1)S(1)} %collective-permute-done.6.refs_0_), channel_id=1, source_target_pairs={{0,4},{4,8},{8,12},{12,16},{16,20},{20,24},{24,28},{28,0},{1,5},{5... | collective-permute-start | bytes 1179656 | tf_op jit(solution)/shard_map/ppermute | solution.py:317
  119.1 8.6 %collective-permute-start.11 = (f32[40,512]{1,0:T(8,128)S(1)}, f32[40,512]{1,0:T(8,128)S(1)}, u32[]{:S(2)}, u32[]{:S(2)}) collective-permute-start(f32[40,512]{1,0:T(8,128)S(1)} %get-tuple-element.32), channel_id=1, source_target_pairs={{0,1},{1,2},{2,3},{3,0},{4,5},{5,6},{6,7},{7,4},{8,9},{9,10},{10,1... | collective-permute-start | bytes 245768 | tf_op jit(solution)/shard_map/ppermute | solution.py:324
  120.4 7.3 %collective-permute-start.12 = (f32[40,512]{1,0:T(8,128)S(1)}, f32[40,512]{1,0:T(8,128)S(1)}, u32[]{:S(2)}, u32[]{:S(2)}) collective-permute-start(f32[40,512]{1,0:T(8,128)S(1)} %get-tuple-element.33), channel_id=1, source_target_pairs={{0,2},{1,3},{2,0},{3,1},{4,6},{5,7},{6,4},{7,5},{8,10},{9,11},{10,... | collective-permute-start | bytes 245768 | tf_op jit(solution)/shard_map/ppermute | solution.py:324
  123.0 4.7 %collective-permute-start.13 = (f32[40,512]{1,0:T(8,128)S(1)}, f32[40,512]{1,0:T(8,128)S(1)}, u32[]{:S(2)}, u32[]{:S(2)}) collective-permute-start(f32[40,512]{1,0:T(8,128)S(1)} %get-tuple-element.34), channel_id=1, source_target_pairs={{0,3},{1,0},{2,1},{3,2},{4,7},{5,4},{6,5},{7,6},{8,11},{9,8},{10,9... | collective-permute-start | bytes 245768 | tf_op jit(solution)/shard_map/ppermute | solution.py:324

commit v2 on v1

--- a/solution.py
+++ b/solution.py
@@ -89,15 +89,56 @@
         block_ref[SPARE - 8 : SPARE + 8, lanes] = jnp.concatenate((above, tile)).astype(jnp.bfloat16)
 
 
+def shard_index():
+    return lax.axis_index("x") * CORE + lax.axis_index("core")
+
+
+def row_starts(lane):
+    first_row = shard_index() * (N // (X * CORE)) + lax.axis_index("z") * ROWS + lane
+    row_at = lax.broadcasted_iota(jnp.int32, (GROUP, 128), 1)
+    spread = lax.broadcasted_iota(jnp.int32, (GROUP, 128), 0) * jnp.int32(668265261)
+    return [
+        (first_row + 128 * k + row_at) * jnp.int32(374761393) + spread
+        for k in range(LANES // 128)
+    ]
+
+
+def product(vectors, bases, starts):
+    parts = [
+        jnp.concatenate([coupling(base + start) for start in starts], axis=1) for base in bases
+    ]
+    return jnp.dot(
+        vectors, jnp.concatenate(parts, axis=0), preferred_element_type=jnp.float32
+    )
+
+
+def shard_kernel(keys_ref, own_ref, out_ref, bases_ref):
+    shard = shard_index()
+    place = lax.axis_index("z") * Y + lax.axis_index("y")
+    steps = lax.broadcasted_iota(jnp.int32, (8, 128), 0) * jnp.int32(GROUP)
+    for k in range(OWN // KEYCOLS):
+        key = keys_ref[0, shard * (OWN // KEYCOLS) + k]
+        columns = place * SEG + shard * OWN + k * KEYCOLS + steps
+        bases_ref[8 * k : 8 * k + 8, :] = key + columns * jnp.int32(668265261)
+
+    def lanes_body(number, carry):
+        lane = pl.multiple_of(number * LANES, LANES)
+        bases = [bases_ref[k : k + 1, :] for k in range(OWN // GROUP)]
+        out_ref[:, pl.ds(lane, LANES)] = product(own_ref[...], bases, row_starts(lane))
+        return carry
+
+    lax.fori_loop(0, Y, lanes_body, 0)
+
+
 def drive_kernel(*refs, shifts, earlier, parts):
     blocks = len(shifts)
     block_refs = refs[:blocks]
-    earlier_refs = refs[blocks : blocks + 2 * earlier]
-    *out_refs, grams_ref, total_ref, vectors_ref, bases_ref = refs[blocks + 2 * earlier :]
+    earlier_refs = refs[blocks : blocks + earlier]
+    *out_refs, grams_ref, total_ref, vectors_ref, bases_ref = refs[blocks + earlier :]
     groups = SEG // GROUP
 
     for slot in range(Z):
-        grams_ref[slot] = earlier_refs[1][slot] if earlier else jnp.zeros((8, 128), jnp.float32)
+        grams_ref[slot] = earlier_refs[1][slot] if earlier == 2 else jnp.zeros((8, 128), jnp.float32)
     steps = lax.broadcasted_iota(jnp.int32, (8, 128), 0) * jnp.int32(GROUP)
     for k, shift in enumerate(shifts):
         place = lax.rem(lax.axis_index("z") + (Z + shift), Z)
@@ -121,32 +162,33 @@
     def part_at(number):
         return lax.rem(lax.axis_index("y") + (parts[0] + number), Y) if parts else number
 
-    first_row = (lax.axis_index("x") * CORE + lax.axis_index("core")) * (N // (X * CORE)) + lax.axis_index("z") * ROWS
-    row_at = lax.broadcasted_iota(jnp.int32, (GROUP, 128), 1)
-    spread = lax.broadcasted_iota(jnp.int32, (GROUP, 128), 0) * jnp.int32(668265261)
-
     def lanes_body(number, carry):
         lane = pl.multiple_of(part_at(number) * LANES, LANES)
-        starts = [
-            (first_row + lane + 128 * k + row_at) * jnp.int32(374761393) + spread
-            for k in range(LANES // 128)
-        ]
+        starts = row_starts(lane)
 
         def body(number, total):
             first = pl.multiple_of(number * groups, groups)
-            parts = []
-            for group in range(groups):
-                base = bases_ref[pl.ds(first + group, 1), :]
-                parts.append(jnp.concatenate([coupling(base + start) for start in starts], axis=1))
-            return total + jnp.dot(
-                vectors_ref[number],
-                jnp.concatenate(parts, axis=0),
-                preferred_element_type=jnp.float32,
-            )
+            bases = [bases_ref[pl.ds(first + group, 1), :] for group in range(groups)]
+            return total + product(vectors_ref[number], bases, starts)
+
+        def others_body(total):
+            shards = [
+                jnp.bitwise_and(shard_index() + shift, X * CORE - 1) for shift in range(1, X * CORE)
+            ]
+            bases = []
+            vectors = []
+            for shard in shards:
+                first = pl.multiple_of(shard * (OWN // GROUP), OWN // GROUP)
+                bases += [bases_ref[pl.ds(first + k, 1), :] for k in range(OWN // GROUP)]
+                vectors.append(vectors_ref[0, :, pl.ds(pl.multiple_of(shard * OWN, OWN), OWN)])
+            return total + product(jnp.concatenate(vectors, axis=1), bases, starts)
 
         here = pl.ds(lane, LANES)
         initial = earlier_refs[0][:, here] if earlier else jnp.zeros((PAD, LANES), jnp.float32)
-        total_ref[:, here] = lax.fori_loop(0, blocks, body, initial)
+        if earlier == 1:
+            total_ref[:, here] = others_body(initial)
+        else:
+            total_ref[:, here] = lax.fori_loop(0, blocks, body, initial)
         return carry
 
     lax.fori_loop(0, len(parts) or Y, lanes_body, 0)
@@ -172,7 +214,7 @@
         out_shape = [drive]
     grams = jax.ShapeDtypeStruct((Z, 8, 128), jnp.float32)
     return pl.pallas_call(
-        functools.partial(drive_kernel, shifts=shifts, earlier=len(earlier) // 2, parts=parts),
+        functools.partial(drive_kernel, shifts=shifts, earlier=len(earlier), parts=parts),
         in_specs=[VMEM] * (count + len(earlier)),
         out_specs=[VMEM] * (len(out_shape) + 1),
         out_shape=out_shape + [grams],
@@ -294,13 +336,21 @@
     own = pl.pallas_call(own_kernel, out_shape=block, compiler_params=PARAMS)(
         tangent, activity.reshape(OWN // 128, 128)
     )
-    mine = jnp.stack(
-        [own]
-        + [
-            lax.ppermute(own, "x", [(i, (i + shift) % X) for i in range(X)])
-            for shift in range(1, X)
-        ]
-    )
+    shards = [
+        lax.ppermute(own, "x", [(i, (i + shift) % X) for i in range(X)]) for shift in range(1, X)
+    ]
+    start = pl.pallas_call(
+        shard_kernel,
+        in_specs=[SMEM, VMEM],
+        out_shape=jax.ShapeDtypeStruct((PAD, ROWS), jnp.float32),
+        scratch_shapes=[pltpu.VMEM((OWN // GROUP, 128), jnp.int32)],
+        cost_estimate=pl.CostEstimate(
+            flops=OWN * ROWS * 1500, bytes_accessed=PAD * OWN * 2, transcendentals=0
+        ),
+        compiler_params=PARAMS,
+    )(block_keys, own)
+    shards, start = lax.optimization_barrier((shards, start))
+    mine = jnp.stack([own] + shards)
     others = lax.ppermute(mine, "core", [(0, 1), (1, 0)])
     near = pl.pallas_call(
         block_kernel,
@@ -312,7 +362,7 @@
     up = [(i, (i + 1) % Z) for i in range(Z)]
     down = [(i, (i - 1) % Z) for i in range(Z)]
     below, above = lax.ppermute(near, "z", up), lax.ppermute(near, "z", down)
-    earlier = partial_drive((0,), [near])
+    earlier = partial_drive((0,), [near], (start,))
     for step in range(1, Z // 2):
         next_below = lax.ppermute(below, "z", up)
         next_above = lax.ppermute(above, "z", down) if step + 1 < Z // 2 else None

time: 161 us -> 158 us (0.981)
  waiting for transfers between devices: 3.18 us -> 1.1 us
  Pallas kernels: 102 us -> 104 us
  starting transfers between devices: 24.4 us -> 22.7 us
    pallas_call x0 -> x1, Pallas kernels: none -> 2.53 us  [per_device(): pl.pallas_call(shard_kernel, in_specs=[SMEM, VMEM], out_shape=jax.ShapeDt...]
    ppermute x2, starting transfers between devices: 5.31 us -> 2.9 us  [per_device(): next_above = lax.ppermute(above, 'z', down) if step + 1 < Z // 2 else None]
    ppermute x3, waiting for transfers between devices: 2.08 us -> 0.01 us  [per_device(): lax.ppermute(own, 'x', [(i, (i + shift) % X) for i in range(X)])]
  transfers between devices with their start and end apart: 14 -> 14, of which waited for: 3 -> 1; matrix products, arithmetic and copies ran while one was open for 0% -> 0% of each run, Pallas kernels for 54% -> 56%
where the time goes in v2:
time: 158 us
  Pallas kernels  104 us (66%)
  blocking collectives  28.2 us (18%)
  starting transfers between devices  22.7 us (14%)
    pallas_call x6, Pallas kernels, partial_drive(): pl.pallas_call(functools.partial(drive_kernel, shifts=shifts, earlier=len...  95.7 us
    all_to_all x1, blocking collectives, gather_grams(): near = jnp.sum(lax.all_to_all(copies, ('x', 'core', 'y'), 0, 0), axis=0)  15.6 us
    all_to_all x1, blocking collectives, gather_grams(): return lax.all_to_all(jnp.broadcast_to(near, (Z, *near.shape)), 'z', 0, 0)  12.7 us
    ppermute x3, starting transfers between devices, per_device(): lax.ppermute(own, 'x', [(i, (i + shift) % X) for i in range(X)])  5.72 us
    ppermute x2, starting transfers between devices, per_device(): below, above = (lax.ppermute(near, 'z', up), lax.ppermute(near, 'z', down))  5.59 us
    ppermute x3, starting transfers between devices, per_device(): lax.ppermute(piece, 'y', [(i, (i + shift) % Y) for i in range(Y)])  4.98 us
  transfers between devices with their start and end apart: 14, of which 1 were waited for; matrix products, arithmetic and copies ran while one was open for 0% of the time, Pallas kernels for 56%

profile of v2, /device:TPU:1, one launch (start us, length us, event | category | flops | bytes accessed | tf_op | source)
XLA Modules:
  0.0 158.0 jit_solution(9626439622318641398)
XLA Ops:
  2.1 2.1 %collective-permute-start = (bf16[48,512]{1,0:T(8,128)(2,1)S(1)}, bf16[48,512]{1,0:T(8,128)(2,1)S(1)}, u32[]{:S(2)}, u32[]{:S(2)}) collective-permute-start(bf16[48,512]{1,0:T(8,128)(2,1)S(1)} %shard_map.66.own_ref), channel_id=1, source_target_pairs={{0,64},{64,128},{128,192},{192,0},{1,65},{65,129},{129,193},{193,1... | collective-permute-start | bytes 147464 | tf_op jit(solution)/shard_map/ppermute | solution.py:340
  4.2 2.5 %collective-permute-start.1 = (bf16[48,512]{1,0:T(8,128)(2,1)S(1)}, bf16[48,512]{1,0:T(8,128)(2,1)S(1)}, u32[]{:S(2)}, u32[]{:S(2)}) collective-permute-start(bf16[48,512]{1,0:T(8,128)(2,1)S(1)} %shard_map.66.own_ref), channel_id=1, source_target_pairs={{0,128},{64,192},{128,0},{192,64},{1,129},{65,193},{129,1},{193,65... | collective-permute-start | bytes 147464 | tf_op jit(solution)/shard_map/ppermute | solution.py:340
  6.7 1.2 collective-permute-start.2
  7.8 2.5 %shard_map.67.refs_1_ = f32[48,2048]{1,0:T(8,128)S(1)} custom-call(s32[1,16]{1,0:T(1,128)S(1)} %copy-done.2, bf16[48,512]{1,0:T(8,128)(2,1)S(1)} %shard_map.66.own_ref), custom_call_target="tpu_custom_call" | custom-call | flops 1572864000 | bytes 49152 | tf_op jit(solution)/shard_map/pallas_call | solution.py:342
  10.4 1.8 %collective-permute-start.3 = (bf16[4,48,512]{2,1,0:T(8,128)(2,1)S(1)}, bf16[4,48,512]{2,1,0:T(8,128)(2,1)S(1)}, u32[]{:S(2)}, u32[]{:S(2)}) collective-permute-start(bf16[4,48,512]{2,1,0:T(8,128)(2,1)S(1)} %pad_maximum_fusion.mine_ref), channel_id=1, source_target_pairs={{0,32},{32,0},{1,33},{33,1},{2,34},{34,2},{3,35},{35,3},{4,36},{36... | collective-permute-start | bytes 589832 | tf_op jit(solution)/shard_map/ppermute | solution.py:354
  12.2 1.1 collective-permute-done.3.others_ref
  13.3 0.9 shard_map.68.refs_0_
  14.1 1.6 collective-permute-start.4
  15.7 4.0 %collective-permute-start.8 = (bf16[48,4096]{1,0:T(8,128)(2,1)S(1)}, bf16[48,4096]{1,0:T(8,128)(2,1)S(1)}, u32[]{:S(2)}, u32[]{:S(2)}) collective-permute-start(bf16[48,4096]{1,0:T(8,128)(2,1)S(1)} %shard_map.68.refs_0_), channel_id=1, source_target_pairs={{0,28},{4,0},{8,4},{12,8},{16,12},{20,16},{24,20},{28,24},{1,29},{... | collective-permute-start | bytes 1179656 | tf_op jit(solution)/shard_map/ppermute | solution.py:364
  19.7 10.6 %shard_map.69 = (f32[48,2048]{1,0:T(8,128)S(1)}, f32[8,8,128]{2,1,0:T(8,128)S(1)}) custom-call(bf16[48,4096]{1,0:T(8,128)(2,1)S(1)} %shard_map.68.refs_0_, f32[48,2048]{1,0:T(8,128)S(1)} %shard_map.67.refs_1_), custom_call_target="tpu_custom_call" | custom-call | flops 12582912000 | bytes 393216 | tf_op jit(solution)/shard_map/pallas_call | solution.py:216
  30.4 2.7 %collective-permute-start.9 = (bf16[48,4096]{1,0:T(8,128)(2,1)S(1)}, bf16[48,4096]{1,0:T(8,128)(2,1)S(1)}, u32[]{:S(2)}, u32[]{:S(2)}) collective-permute-start(bf16[48,4096]{1,0:T(8,128)(2,1)S(1)} %collective-permute-done.8.refs_1_), channel_id=1, source_target_pairs={{0,28},{4,0},{8,4},{12,8},{16,12},{20,16},{24,20},{28,24},{1,29},{... | collective-permute-start | bytes 1179656 | tf_op jit(solution)/shard_map/ppermute | solution.py:368
  33.1 24.0 %shard_map.70 = (f32[48,2048]{1,0:T(8,128)S(1)}, f32[8,8,128]{2,1,0:T(8,128)S(1)}) custom-call(bf16[48,4096]{1,0:T(8,128)(2,1)S(1)} %collective-permute-done.4.refs_0_, bf16[48,4096]{1,0:T(8,128)(2,1)S(1)} %collective-permute-done.8.refs_1_, f32[48,2048]{1,0:T(8,128)S(1)} %get-tuple-element.31.refs_2_, f32[8,8,128]{2,1,0:T(8,128)S(1)} %get-tuple-element.32.refs_3_), custom_call_target="tpu_custom_call" | custom-call | flops 25165824000 | bytes 786432 | tf_op jit(solution)/shard_map/pallas_call | solution.py:216
  57.3 1.3 collective-permute-start.6
  58.6 24.0 %shard_map.71 = (f32[48,2048]{1,0:T(8,128)S(1)}, f32[8,8,128]{2,1,0:T(8,128)S(1)}) custom-call(bf16[48,4096]{1,0:T(8,128)(2,1)S(1)} %collective-permute-done.5.refs_0_, bf16[48,4096]{1,0:T(8,128)(2,1)S(1)} %collective-permute-done.9.refs_1_, f32[48,2048]{1,0:T(8,128)S(1)} %get-tuple-element.33.refs_2_, f32[8,8,128]{2,1,0:T(8,128)S(1)} %get-tuple-element.34.refs_3_), custom_call_target="tpu_custom_call" | custom-call | flops 25165824000 | bytes 786432 | tf_op jit(solution)/shard_map/pallas_call | solution.py:216
  82.9 24.0 %shard_map.72 = (f32[48,2048]{1,0:T(8,128)S(1)}, f32[8,8,128]{2,1,0:T(8,128)S(1)}) custom-call(bf16[48,4096]{1,0:T(8,128)(2,1)S(1)} %collective-permute-done.6.refs_0_, bf16[48,4096]{1,0:T(8,128)(2,1)S(1)} %collective-permute-done.10.refs_1_, f32[48,2048]{1,0:T(8,128)S(1)} %get-tuple-element.35.refs_2_, f32[8,8,128]{2,1,0:T(8,128)S(1)} %get-tuple-element.36.refs_3_), custom_call_target="tpu_custom_call" | custom-call | flops 25165824000 | bytes 786432 | tf_op jit(solution)/shard_map/pallas_call | solution.py:216
  106.9 9.6 %shard_map.74 = (f32[40,512]{1,0:T(8,128)S(1)}, f32[40,512]{1,0:T(8,128)S(1)}, f32[40,512]{1,0:T(8,128)S(1)}, f32[8,8,128]{2,1,0:T(8,128)}) custom-call(bf16[48,4096]{1,0:T(8,128)(2,1)S(1)} %collective-permute-done.7.refs_0_, f32[48,2048]{1,0:T(8,128)S(1)} %get-tuple-element.37.refs_1_, f32[8,8,128]{2,1,0:T(8,128)S(1)} %get-tuple-element.38.refs_2_), custom_call_target="tpu_custom_call" | custom-call | flops 9437184000 | bytes 393216 | tf_op jit(solution)/shard_map/pallas_call | solution.py:216
  116.6 1.3 collective-permute-start.11
  117.9 2.6 %collective-permute-start.12 = (f32[40,512]{1,0:T(8,128)S(1)}, f32[40,512]{1,0:T(8,128)S(1)}, u32[]{:S(2)}, u32[]{:S(2)}) collective-permute-start(f32[40,512]{1,0:T(8,128)S(1)} %get-tuple-element.41), channel_id=1, source_target_pairs={{0,2},{1,3},{2,0},{3,1},{4,6},{5,7},{6,4},{7,5},{8,10},{9,11},{10,... | collective-permute-start | bytes 245768 | tf_op jit(solution)/shard_map/ppermute | solution.py:374
  120.5 1.1 collective-permute-start.13
  121.6 3.6 %shard_map.73 = (f32[40,512]{1,0:T(8,128)S(1)}, f32[8,8,128]{2,1,0:T(8,128)}) custom-call(bf16[48,4096]{1,0:T(8,128)(2,1)S(1)} %collective-permute-done.7.refs_0_, f32[48,2048]{1,0:T(8,128)S(1)} %get-tuple-element.37.refs_1_, f32[8,8,128]{2,1,0:T(8,128)S(1)} %get-tuple-element.38.refs_2_), custom_call_target="tpu_custom_call" | custom-call | flops 3145728000 | bytes 393216 | tf_op jit(solution)/shard_map/pallas_call | solution.py:216
  125.2 1.8 %shard_map.75 = (f32[1,512]{1,0:T(1,128)}, f32[32,512]{1,0:T(8,128)S(1)}, f32[32,8,128]{2,1,0:T(8,128)S(1)}, f32[32,32]{1,0:T(8,128)S(1)}) custom-call(f32[40,512]{1,0:T(8,128)S(1)} %get-tuple-element.39.mine_ref, f32[40,512]{1,0:T(8,128)S(1)} %collective-permute-done.11.others_ref, f32[40,512]{1,0:T(8,128)S(1)} %collective-permute-done.12.refs_0_, ...), custom_call_target="tpu_custom_call" | custom-call | tf_op jit(solution)/shard_map/pallas_call | solution.py:380
  127.0 15.6 %all_to_all.10 = f32[32,8,128]{2,1,0:T(8,128)S(1)} all-to-all(f32[32,8,128]{2,1,0:T(8,128)S(1)} %get-tuple-element.43), channel_id=1, replica_groups=mesh['x'=4,'core'=2,'z'=8,'y'=4] {'x','core','y'}, dimensions={0} | all-to-all | bytes 262144 | tf_op jit(solution)/shard_map/all_to_all | solution.py:330
  142.6 12.7 %all_to_all.11.grams_ref = f32[8,8,128]{2,1,0:T(8,128)S(1)} all-to-all(f32[8,8,128]{2,1,0:T(8,128)S(1)} %broadcast_in_dim.3), channel_id=1, replica_groups=mesh['x'=4,'core'=2,'z'=8,'y'=4] {'z'}, dimensions={0} | all-to-all | bytes 65536 | tf_op jit(solution)/shard_map/all_to_all | solution.py:331
  155.3 2.7 %shard_map.76 = (f32[32,512]{1,0:T(8,128)}, f32[32,32]{1,0:T(8,128)}, f32[32,32]{1,0:T(8,128)}) custom-call(f32[8,8,128]{2,1,0:T(8,128)S(1)} %all_to_all.11.grams_ref, f32[32,512]{1,0:T(8,128)S(1)} %get-tuple-element.44.scaled_ref, f32[32,32]{1,0:T(8,128)S(1)} %get-tuple-element.45.input_upper_ref), custom_call_target="tpu_custom_call" | custom-call | tf_op jit(solution)/shard_map/pallas_call | solution.py:391
  (26 shorter events, 2.2 us)
Async XLA Ops:
  0.6 0.7 copy-start.1
  1.3 0.8 copy-start
  2.1 5.7 %copy-start.2 = (s32[1,16]{1,0:T(1,128)S(1)}, s32[1,16]{1,0:T(1,128)}, u32[]{:S(2)}) copy-start(s32[1,16]{1,0:T(1,128)} %keys_ref.3) | copy-start | bytes 196
  2.1 8.3 %collective-permute-start = (bf16[48,512]{1,0:T(8,128)(2,1)S(1)}, bf16[48,512]{1,0:T(8,128)(2,1)S(1)}, u32[]{:S(2)}, u32[]{:S(2)}) collective-permute-start(bf16[48,512]{1,0:T(8,128)(2,1)S(1)} %shard_map.66.own_ref), channel_id=1, source_target_pairs={{0,64},{64,128},{128,192},{192,0},{1,65},{65,129},{129,193},{193,1... | collective-permute-start | bytes 147464 | tf_op jit(solution)/shard_map/ppermute | solution.py:340
  4.2 6.2 %collective-permute-start.1 = (bf16[48,512]{1,0:T(8,128)(2,1)S(1)}, bf16[48,512]{1,0:T(8,128)(2,1)S(1)}, u32[]{:S(2)}, u32[]{:S(2)}) collective-permute-start(bf16[48,512]{1,0:T(8,128)(2,1)S(1)} %shard_map.66.own_ref), channel_id=1, source_target_pairs={{0,128},{64,192},{128,0},{192,64},{1,129},{65,193},{129,1},{193,65... | collective-permute-start | bytes 147464 | tf_op jit(solution)/shard_map/ppermute | solution.py:340
  6.7 3.7 %collective-permute-start.2 = (bf16[48,512]{1,0:T(8,128)(2,1)S(1)}, bf16[48,512]{1,0:T(8,128)(2,1)S(1)}, u32[]{:S(2)}, u32[]{:S(2)}) collective-permute-start(bf16[48,512]{1,0:T(8,128)(2,1)S(1)} %shard_map.66.own_ref), channel_id=1, source_target_pairs={{0,192},{64,0},{128,64},{192,128},{1,193},{65,1},{129,65},{193,129... | collective-permute-start | bytes 147464 | tf_op jit(solution)/shard_map/ppermute | solution.py:340
  10.4 2.9 %collective-permute-start.3 = (bf16[4,48,512]{2,1,0:T(8,128)(2,1)S(1)}, bf16[4,48,512]{2,1,0:T(8,128)(2,1)S(1)}, u32[]{:S(2)}, u32[]{:S(2)}) collective-permute-start(bf16[4,48,512]{2,1,0:T(8,128)(2,1)S(1)} %pad_maximum_fusion.mine_ref), channel_id=1, source_target_pairs={{0,32},{32,0},{1,33},{33,1},{2,34},{34,2},{3,35},{35,3},{4,36},{36... | collective-permute-start | bytes 589832 | tf_op jit(solution)/shard_map/ppermute | solution.py:354
  14.1 16.2 %collective-permute-start.4 = (bf16[48,4096]{1,0:T(8,128)(2,1)S(1)}, bf16[48,4096]{1,0:T(8,128)(2,1)S(1)}, u32[]{:S(2)}, u32[]{:S(2)}) collective-permute-start(bf16[48,4096]{1,0:T(8,128)(2,1)S(1)} %shard_map.68.refs_0_), channel_id=1, source_target_pairs={{0,4},{4,8},{8,12},{12,16},{16,20},{20,24},{24,28},{28,0},{1,5},{5... | collective-permute-start | bytes 1179656 | tf_op jit(solution)/shard_map/ppermute | solution.py:364
  15.7 14.7 %collective-permute-start.8 = (bf16[48,4096]{1,0:T(8,128)(2,1)S(1)}, bf16[48,4096]{1,0:T(8,128)(2,1)S(1)}, u32[]{:S(2)}, u32[]{:S(2)}) collective-permute-start(bf16[48,4096]{1,0:T(8,128)(2,1)S(1)} %shard_map.68.refs_0_), channel_id=1, source_target_pairs={{0,28},{4,0},{8,4},{12,8},{16,12},{20,16},{24,20},{28,24},{1,29},{... | collective-permute-start | bytes 1179656 | tf_op jit(solution)/shard_map/ppermute | solution.py:364
  30.3 27.0 %collective-permute-start.5 = (bf16[48,4096]{1,0:T(8,128)(2,1)S(1)}, bf16[48,4096]{1,0:T(8,128)(2,1)S(1)}, u32[]{:S(2)}, u32[]{:S(2)}) collective-permute-start(bf16[48,4096]{1,0:T(8,128)(2,1)S(1)} %collective-permute-done.4.refs_0_), channel_id=1, source_target_pairs={{0,4},{4,8},{8,12},{12,16},{16,20},{20,24},{24,28},{28,0},{1,5},{5... | collective-permute-start | bytes 1179656 | tf_op jit(solution)/shard_map/ppermute | solution.py:367
  30.4 26.6 %collective-permute-start.9 = (bf16[48,4096]{1,0:T(8,128)(2,1)S(1)}, bf16[48,4096]{1,0:T(8,128)(2,1)S(1)}, u32[]{:S(2)}, u32[]{:S(2)}) collective-permute-start(bf16[48,4096]{1,0:T(8,128)(2,1)S(1)} %collective-permute-done.8.refs_1_), channel_id=1, source_target_pairs={{0,28},{4,0},{8,4},{12,8},{16,12},{20,16},{24,20},{28,24},{1,29},{... | collective-permute-start | bytes 1179656 | tf_op jit(solution)/shard_map/ppermute | solution.py:368
  57.1 25.9 %collective-permute-start.10 = (bf16[48,4096]{1,0:T(8,128)(2,1)S(1)}, bf16[48,4096]{1,0:T(8,128)(2,1)S(1)}, u32[]{:S(2)}, u32[]{:S(2)}) collective-permute-start(bf16[48,4096]{1,0:T(8,128)(2,1)S(1)} %collective-permute-done.9.refs_1_), channel_id=1, source_target_pairs={{0,28},{4,0},{8,4},{12,8},{16,12},{20,16},{24,20},{28,24},{1,29},{... | collective-permute-start | bytes 1179656 | tf_op jit(solution)/shard_map/ppermute | solution.py:368
  57.3 25.3 %collective-permute-start.6 = (bf16[48,4096]{1,0:T(8,128)(2,1)S(1)}, bf16[48,4096]{1,0:T(8,128)(2,1)S(1)}, u32[]{:S(2)}, u32[]{:S(2)}) collective-permute-start(bf16[48,4096]{1,0:T(8,128)(2,1)S(1)} %collective-permute-done.5.refs_0_), channel_id=1, source_target_pairs={{0,4},{4,8},{8,12},{12,16},{16,20},{20,24},{24,28},{28,0},{1,5},{5... | collective-permute-start | bytes 1179656 | tf_op jit(solution)/shard_map/ppermute | solution.py:367
  82.6 24.3 %collective-permute-start.7 = (bf16[48,4096]{1,0:T(8,128)(2,1)S(1)}, bf16[48,4096]{1,0:T(8,128)(2,1)S(1)}, u32[]{:S(2)}, u32[]{:S(2)}) collective-permute-start(bf16[48,4096]{1,0:T(8,128)(2,1)S(1)} %collective-permute-done.6.refs_0_), channel_id=1, source_target_pairs={{0,4},{4,8},{8,12},{12,16},{16,20},{20,24},{24,28},{28,0},{1,5},{5... | collective-permute-start | bytes 1179656 | tf_op jit(solution)/shard_map/ppermute | solution.py:367
  116.6 8.6 %collective-permute-start.11 = (f32[40,512]{1,0:T(8,128)S(1)}, f32[40,512]{1,0:T(8,128)S(1)}, u32[]{:S(2)}, u32[]{:S(2)}) collective-permute-start(f32[40,512]{1,0:T(8,128)S(1)} %get-tuple-element.40), channel_id=1, source_target_pairs={{0,1},{1,2},{2,3},{3,0},{4,5},{5,6},{6,7},{7,4},{8,9},{9,10},{10,1... | collective-permute-start | bytes 245768 | tf_op jit(solution)/shard_map/ppermute | solution.py:374
  117.9 7.3 %collective-permute-start.12 = (f32[40,512]{1,0:T(8,128)S(1)}, f32[40,512]{1,0:T(8,128)S(1)}, u32[]{:S(2)}, u32[]{:S(2)}) collective-permute-start(f32[40,512]{1,0:T(8,128)S(1)} %get-tuple-element.41), channel_id=1, source_target_pairs={{0,2},{1,3},{2,0},{3,1},{4,6},{5,7},{6,4},{7,5},{8,10},{9,11},{10,... | collective-permute-start | bytes 245768 | tf_op jit(solution)/shard_map/ppermute | solution.py:374
  120.5 4.7 %collective-permute-start.13 = (f32[40,512]{1,0:T(8,128)S(1)}, f32[40,512]{1,0:T(8,128)S(1)}, u32[]{:S(2)}, u32[]{:S(2)}) collective-permute-start(f32[40,512]{1,0:T(8,128)S(1)} %get-tuple-element.42), channel_id=1, source_target_pairs={{0,3},{1,0},{2,1},{3,2},{4,7},{5,4},{6,5},{7,6},{8,11},{9,8},{10,9... | collective-permute-start | bytes 245768 | tf_op jit(solution)/shard_map/ppermute | solution.py:374

commit v3 on v2

--- a/solution.py
+++ b/solution.py
@@ -130,7 +130,7 @@
     lax.fori_loop(0, Y, lanes_body, 0)
 
 
-def drive_kernel(*refs, shifts, earlier, parts):
+def drive_kernel(*refs, shifts, earlier, parts, unroll):
     blocks = len(shifts)
     block_refs = refs[:blocks]
     earlier_refs = refs[blocks : blocks + earlier]
@@ -162,16 +162,11 @@
     def part_at(number):
         return lax.rem(lax.axis_index("y") + (parts[0] + number), Y) if parts else number
 
-    def lanes_body(number, carry):
+    def step_body(step, carry):
+        number, block = lax.shift_right_logical(step, blocks - 1), jnp.bitwise_and(step, blocks - 1)
         lane = pl.multiple_of(part_at(number) * LANES, LANES)
-        starts = row_starts(lane)
-
-        def body(number, total):
-            first = pl.multiple_of(number * groups, groups)
-            bases = [bases_ref[pl.ds(first + group, 1), :] for group in range(groups)]
-            return total + product(vectors_ref[number], bases, starts)
-
-        def others_body(total):
+        here = pl.ds(lane, LANES)
+        if earlier == 1:
             shards = [
                 jnp.bitwise_and(shard_index() + shift, X * CORE - 1) for shift in range(1, X * CORE)
             ]
@@ -181,17 +176,16 @@
                 first = pl.multiple_of(shard * (OWN // GROUP), OWN // GROUP)
                 bases += [bases_ref[pl.ds(first + k, 1), :] for k in range(OWN // GROUP)]
                 vectors.append(vectors_ref[0, :, pl.ds(pl.multiple_of(shard * OWN, OWN), OWN)])
-            return total + product(jnp.concatenate(vectors, axis=1), bases, starts)
-
-        here = pl.ds(lane, LANES)
-        initial = earlier_refs[0][:, here] if earlier else jnp.zeros((PAD, LANES), jnp.float32)
-        if earlier == 1:
-            total_ref[:, here] = others_body(initial)
+            vectors = jnp.concatenate(vectors, axis=1)
         else:
-            total_ref[:, here] = lax.fori_loop(0, blocks, body, initial)
+            first = pl.multiple_of(block * groups, groups)
+            bases = [bases_ref[pl.ds(first + group, 1), :] for group in range(groups)]
+            vectors = vectors_ref[block]
+        total_ref[:, here] += product(vectors, bases, row_starts(lane))
         return carry
 
-    lax.fori_loop(0, len(parts) or Y, lanes_body, 0)
+    total_ref[...] = earlier_refs[0][...]
+    lax.fori_loop(0, (len(parts) or Y) * blocks, step_body, 0, unroll=unroll)
     if not parts:
         out_refs[0][...] = total_ref[...]
         return
@@ -205,7 +199,7 @@
         out_ref[GRAM_ROW:, 128:256] = gram[4:]
 
 
-def partial_drive(shifts, blocks, earlier=(), parts=()):
+def partial_drive(shifts, blocks, earlier=(), parts=(), unroll=1):
     count = len(blocks)
     drive = jax.ShapeDtypeStruct((PAD, ROWS), jnp.float32)
     if parts:
@@ -214,7 +208,9 @@
         out_shape = [drive]
     grams = jax.ShapeDtypeStruct((Z, 8, 128), jnp.float32)
     return pl.pallas_call(
-        functools.partial(drive_kernel, shifts=shifts, earlier=len(earlier), parts=parts),
+        functools.partial(
+            drive_kernel, shifts=shifts, earlier=len(earlier), parts=parts, unroll=unroll
+        ),
         in_specs=[VMEM] * (count + len(earlier)),
         out_specs=[VMEM] * (len(out_shape) + 1),
         out_shape=out_shape + [grams],
@@ -270,7 +266,7 @@
                 column = column - ratios[m] * element
             pivot = jnp.broadcast_to(column[at : at + 1], wide)
             if floor:
-                least = jnp.maximum(floor * gram[at : at + 1, at : at + 1], 1e-30)
+                least = jnp.maximum(floor * gram[at : at + 1, at : at + 1], 1e-37)
                 pivot = jnp.maximum(pivot, least)
             ratios.append(jnp.where(row_at > at, column / pivot, 0.0))
             scales = jnp.where(row_at == at, lax.rsqrt(pivot), scales)
@@ -366,7 +362,8 @@
     for step in range(1, Z // 2):
         next_below = lax.ppermute(below, "z", up)
         next_above = lax.ppermute(above, "z", down) if step + 1 < Z // 2 else None
-        earlier = partial_drive((-step, step), [below, above], earlier)
+        unroll = 2 if step == 1 else 1
+        earlier = partial_drive((-step, step), [below, above], earlier, unroll=unroll)
         below, above = next_below, next_above
     *sent, _ = partial_drive((Z // 2,), [below], earlier, tuple(range(1, Y)))
     kept, _ = partial_drive((Z // 2,), [below], earlier, (0,))

time: 158 us -> 158 us (level)
  no operation moved by 1% of the time
where the time goes in v3:
time: 158 us; the launch traced here: 157 us
  Pallas kernels  103 us (65%)
  blocking collectives  28.2 us (18%)
  starting transfers between devices  22.7 us (14%)
    pallas_call x6, Pallas kernels, partial_drive(): pl.pallas_call(functools.partial(drive_kernel, shifts=shifts, earlier=len...  95.3 us
    all_to_all x1, blocking collectives, gather_grams(): near = jnp.sum(lax.all_to_all(copies, ('x', 'core', 'y'), 0, 0), axis=0)  15.5 us
    all_to_all x1, blocking collectives, gather_grams(): return lax.all_to_all(jnp.broadcast_to(near, (Z, *near.shape)), 'z', 0, 0)  12.7 us
    ppermute x3, starting transfers between devices, per_device(): lax.ppermute(own, 'x', [(i, (i + shift) % X) for i in range(X)])  5.72 us
    ppermute x2, starting transfers between devices, per_device(): below, above = (lax.ppermute(near, 'z', up), lax.ppermute(near, 'z', down))  5.59 us
    ppermute x3, starting transfers between devices, per_device(): lax.ppermute(piece, 'y', [(i, (i + shift) % Y) for i in range(Y)])  4.98 us
  transfers between devices with their start and end apart: 14, of which 1 were waited for; matrix products, arithmetic and copies ran while one was open for 0% of the time, Pallas kernels for 56%

profile of v3, /device:TPU:1, one launch (start us, length us, event | category | flops | bytes accessed | tf_op | source)
XLA Modules:
  0.0 157.5 jit_solution(15590512627060081213)
XLA Ops:
  2.1 2.1 %collective-permute-start = (bf16[48,512]{1,0:T(8,128)(2,1)S(1)}, bf16[48,512]{1,0:T(8,128)(2,1)S(1)}, u32[]{:S(2)}, u32[]{:S(2)}) collective-permute-start(bf16[48,512]{1,0:T(8,128)(2,1)S(1)} %shard_map.66.own_ref), channel_id=1, source_target_pairs={{0,64},{64,128},{128,192},{192,0},{1,65},{65,129},{129,193},{193,1... | collective-permute-start | bytes 147464 | tf_op jit(solution)/shard_map/ppermute | solution.py:336
  4.2 2.5 %collective-permute-start.1 = (bf16[48,512]{1,0:T(8,128)(2,1)S(1)}, bf16[48,512]{1,0:T(8,128)(2,1)S(1)}, u32[]{:S(2)}, u32[]{:S(2)}) collective-permute-start(bf16[48,512]{1,0:T(8,128)(2,1)S(1)} %shard_map.66.own_ref), channel_id=1, source_target_pairs={{0,128},{64,192},{128,0},{192,64},{1,129},{65,193},{129,1},{193,65... | collective-permute-start | bytes 147464 | tf_op jit(solution)/shard_map/ppermute | solution.py:336
  6.7 1.2 collective-permute-start.2
  7.8 2.5 %shard_map.67.refs_1_ = f32[48,2048]{1,0:T(8,128)S(1)} custom-call(s32[1,16]{1,0:T(1,128)S(1)} %copy-done.2, bf16[48,512]{1,0:T(8,128)(2,1)S(1)} %shard_map.66.own_ref), custom_call_target="tpu_custom_call" | custom-call | flops 1572864000 | bytes 49152 | tf_op jit(solution)/shard_map/pallas_call | solution.py:338
  10.4 1.8 %collective-permute-start.3 = (bf16[4,48,512]{2,1,0:T(8,128)(2,1)S(1)}, bf16[4,48,512]{2,1,0:T(8,128)(2,1)S(1)}, u32[]{:S(2)}, u32[]{:S(2)}) collective-permute-start(bf16[4,48,512]{2,1,0:T(8,128)(2,1)S(1)} %pad_maximum_fusion.mine_ref), channel_id=1, source_target_pairs={{0,32},{32,0},{1,33},{33,1},{2,34},{34,2},{3,35},{35,3},{4,36},{36... | collective-permute-start | bytes 589832 | tf_op jit(solution)/shard_map/ppermute | solution.py:350
  12.2 1.1 collective-permute-done.3.others_ref
  13.3 0.9 shard_map.68.refs_0_
  14.1 1.6 collective-permute-start.4
  15.7 4.0 %collective-permute-start.8 = (bf16[48,4096]{1,0:T(8,128)(2,1)S(1)}, bf16[48,4096]{1,0:T(8,128)(2,1)S(1)}, u32[]{:S(2)}, u32[]{:S(2)}) collective-permute-start(bf16[48,4096]{1,0:T(8,128)(2,1)S(1)} %shard_map.68.refs_0_), channel_id=1, source_target_pairs={{0,28},{4,0},{8,4},{12,8},{16,12},{20,16},{24,20},{28,24},{1,29},{... | collective-permute-start | bytes 1179656 | tf_op jit(solution)/shard_map/ppermute | solution.py:360
  19.7 10.6 %shard_map.69 = (f32[48,2048]{1,0:T(8,128)S(1)}, f32[8,8,128]{2,1,0:T(8,128)S(1)}) custom-call(bf16[48,4096]{1,0:T(8,128)(2,1)S(1)} %shard_map.68.refs_0_, f32[48,2048]{1,0:T(8,128)S(1)} %shard_map.67.refs_1_), custom_call_target="tpu_custom_call" | custom-call | flops 12582912000 | bytes 393216 | tf_op jit(solution)/shard_map/pallas_call | solution.py:210
  30.4 2.7 %collective-permute-start.9 = (bf16[48,4096]{1,0:T(8,128)(2,1)S(1)}, bf16[48,4096]{1,0:T(8,128)(2,1)S(1)}, u32[]{:S(2)}, u32[]{:S(2)}) collective-permute-start(bf16[48,4096]{1,0:T(8,128)(2,1)S(1)} %collective-permute-done.8.refs_1_), channel_id=1, source_target_pairs={{0,28},{4,0},{8,4},{12,8},{16,12},{20,16},{24,20},{28,24},{1,29},{... | collective-permute-start | bytes 1179656 | tf_op jit(solution)/shard_map/ppermute | solution.py:364
  33.1 23.4 %shard_map.70 = (f32[48,2048]{1,0:T(8,128)S(1)}, f32[8,8,128]{2,1,0:T(8,128)S(1)}) custom-call(bf16[48,4096]{1,0:T(8,128)(2,1)S(1)} %collective-permute-done.4.refs_0_, bf16[48,4096]{1,0:T(8,128)(2,1)S(1)} %collective-permute-done.8.refs_1_, f32[48,2048]{1,0:T(8,128)S(1)} %get-tuple-element.31.refs_2_, f32[8,8,128]{2,1,0:T(8,128)S(1)} %get-tuple-element.32.refs_3_), custom_call_target="tpu_custom_call" | custom-call | flops 25165824000 | bytes 786432 | tf_op jit(solution)/shard_map/pallas_call | solution.py:210
  56.8 1.3 collective-permute-start.6
  58.1 24.0 %shard_map.71 = (f32[48,2048]{1,0:T(8,128)S(1)}, f32[8,8,128]{2,1,0:T(8,128)S(1)}) custom-call(bf16[48,4096]{1,0:T(8,128)(2,1)S(1)} %collective-permute-done.5.refs_0_, bf16[48,4096]{1,0:T(8,128)(2,1)S(1)} %collective-permute-done.9.refs_1_, f32[48,2048]{1,0:T(8,128)S(1)} %get-tuple-element.33.refs_2_, f32[8,8,128]{2,1,0:T(8,128)S(1)} %get-tuple-element.34.refs_3_), custom_call_target="tpu_custom_call" | custom-call | flops 25165824000 | bytes 786432 | tf_op jit(solution)/shard_map/pallas_call | solution.py:210
  82.4 24.0 %shard_map.72 = (f32[48,2048]{1,0:T(8,128)S(1)}, f32[8,8,128]{2,1,0:T(8,128)S(1)}) custom-call(bf16[48,4096]{1,0:T(8,128)(2,1)S(1)} %collective-permute-done.6.refs_0_, bf16[48,4096]{1,0:T(8,128)(2,1)S(1)} %collective-permute-done.10.refs_1_, f32[48,2048]{1,0:T(8,128)S(1)} %get-tuple-element.35.refs_2_, f32[8,8,128]{2,1,0:T(8,128)S(1)} %get-tuple-element.36.refs_3_), custom_call_target="tpu_custom_call" | custom-call | flops 25165824000 | bytes 786432 | tf_op jit(solution)/shard_map/pallas_call | solution.py:210
  106.5 9.7 %shard_map.74 = (f32[40,512]{1,0:T(8,128)S(1)}, f32[40,512]{1,0:T(8,128)S(1)}, f32[40,512]{1,0:T(8,128)S(1)}, f32[8,8,128]{2,1,0:T(8,128)}) custom-call(bf16[48,4096]{1,0:T(8,128)(2,1)S(1)} %collective-permute-done.7.refs_0_, f32[48,2048]{1,0:T(8,128)S(1)} %get-tuple-element.37.refs_1_, f32[8,8,128]{2,1,0:T(8,128)S(1)} %get-tuple-element.38.refs_2_), custom_call_target="tpu_custom_call" | custom-call | flops 9437184000 | bytes 393216 | tf_op jit(solution)/shard_map/pallas_call | solution.py:210
  116.1 1.3 collective-permute-start.11
  117.4 2.6 %collective-permute-start.12 = (f32[40,512]{1,0:T(8,128)S(1)}, f32[40,512]{1,0:T(8,128)S(1)}, u32[]{:S(2)}, u32[]{:S(2)}) collective-permute-start(f32[40,512]{1,0:T(8,128)S(1)} %get-tuple-element.41), channel_id=1, source_target_pairs={{0,2},{1,3},{2,0},{3,1},{4,6},{5,7},{6,4},{7,5},{8,10},{9,11},{10,... | collective-permute-start | bytes 245768 | tf_op jit(solution)/shard_map/ppermute | solution.py:371
  120.0 1.1 collective-permute-start.13
  121.1 3.6 %shard_map.73 = (f32[40,512]{1,0:T(8,128)S(1)}, f32[8,8,128]{2,1,0:T(8,128)}) custom-call(bf16[48,4096]{1,0:T(8,128)(2,1)S(1)} %collective-permute-done.7.refs_0_, f32[48,2048]{1,0:T(8,128)S(1)} %get-tuple-element.37.refs_1_, f32[8,8,128]{2,1,0:T(8,128)S(1)} %get-tuple-element.38.refs_2_), custom_call_target="tpu_custom_call" | custom-call | flops 3145728000 | bytes 393216 | tf_op jit(solution)/shard_map/pallas_call | solution.py:210
  124.7 1.8 %shard_map.75 = (f32[1,512]{1,0:T(1,128)}, f32[32,512]{1,0:T(8,128)S(1)}, f32[32,8,128]{2,1,0:T(8,128)S(1)}, f32[32,32]{1,0:T(8,128)S(1)}) custom-call(f32[40,512]{1,0:T(8,128)S(1)} %get-tuple-element.39.mine_ref, f32[40,512]{1,0:T(8,128)S(1)} %collective-permute-done.11.others_ref, f32[40,512]{1,0:T(8,128)S(1)} %collective-permute-done.12.refs_0_, ...), custom_call_target="tpu_custom_call" | custom-call | tf_op jit(solution)/shard_map/pallas_call | solution.py:377
  126.5 15.5 %all_to_all.10 = f32[32,8,128]{2,1,0:T(8,128)S(1)} all-to-all(f32[32,8,128]{2,1,0:T(8,128)S(1)} %get-tuple-element.43), channel_id=1, replica_groups=mesh['x'=4,'core'=2,'z'=8,'y'=4] {'x','core','y'}, dimensions={0} | all-to-all | bytes 262144 | tf_op jit(solution)/shard_map/all_to_all | solution.py:326
  142.1 12.7 %all_to_all.11.grams_ref = f32[8,8,128]{2,1,0:T(8,128)S(1)} all-to-all(f32[8,8,128]{2,1,0:T(8,128)S(1)} %broadcast_in_dim.3), channel_id=1, replica_groups=mesh['x'=4,'core'=2,'z'=8,'y'=4] {'z'}, dimensions={0} | all-to-all | bytes 65536 | tf_op jit(solution)/shard_map/all_to_all | solution.py:327
  154.8 2.7 %shard_map.76 = (f32[32,512]{1,0:T(8,128)}, f32[32,32]{1,0:T(8,128)}, f32[32,32]{1,0:T(8,128)}) custom-call(f32[8,8,128]{2,1,0:T(8,128)S(1)} %all_to_all.11.grams_ref, f32[32,512]{1,0:T(8,128)S(1)} %get-tuple-element.44.scaled_ref, f32[32,32]{1,0:T(8,128)S(1)} %get-tuple-element.45.input_upper_ref), custom_call_target="tpu_custom_call" | custom-call | tf_op jit(solution)/shard_map/pallas_call | solution.py:388
  (26 shorter events, 2.2 us)
Async XLA Ops:
  0.6 0.7 copy-start.1
  1.3 0.8 copy-start
  2.1 5.7 %copy-start.2 = (s32[1,16]{1,0:T(1,128)S(1)}, s32[1,16]{1,0:T(1,128)}, u32[]{:S(2)}) copy-start(s32[1,16]{1,0:T(1,128)} %keys_ref.3) | copy-start | bytes 196
  2.1 8.3 %collective-permute-start = (bf16[48,512]{1,0:T(8,128)(2,1)S(1)}, bf16[48,512]{1,0:T(8,128)(2,1)S(1)}, u32[]{:S(2)}, u32[]{:S(2)}) collective-permute-start(bf16[48,512]{1,0:T(8,128)(2,1)S(1)} %shard_map.66.own_ref), channel_id=1, source_target_pairs={{0,64},{64,128},{128,192},{192,0},{1,65},{65,129},{129,193},{193,1... | collective-permute-start | bytes 147464 | tf_op jit(solution)/shard_map/ppermute | solution.py:336
  4.2 6.2 %collective-permute-start.1 = (bf16[48,512]{1,0:T(8,128)(2,1)S(1)}, bf16[48,512]{1,0:T(8,128)(2,1)S(1)}, u32[]{:S(2)}, u32[]{:S(2)}) collective-permute-start(bf16[48,512]{1,0:T(8,128)(2,1)S(1)} %shard_map.66.own_ref), channel_id=1, source_target_pairs={{0,128},{64,192},{128,0},{192,64},{1,129},{65,193},{129,1},{193,65... | collective-permute-start | bytes 147464 | tf_op jit(solution)/shard_map/ppermute | solution.py:336
  6.7 3.7 %collective-permute-start.2 = (bf16[48,512]{1,0:T(8,128)(2,1)S(1)}, bf16[48,512]{1,0:T(8,128)(2,1)S(1)}, u32[]{:S(2)}, u32[]{:S(2)}) collective-permute-start(bf16[48,512]{1,0:T(8,128)(2,1)S(1)} %shard_map.66.own_ref), channel_id=1, source_target_pairs={{0,192},{64,0},{128,64},{192,128},{1,193},{65,1},{129,65},{193,129... | collective-permute-start | bytes 147464 | tf_op jit(solution)/shard_map/ppermute | solution.py:336
  10.4 2.9 %collective-permute-start.3 = (bf16[4,48,512]{2,1,0:T(8,128)(2,1)S(1)}, bf16[4,48,512]{2,1,0:T(8,128)(2,1)S(1)}, u32[]{:S(2)}, u32[]{:S(2)}) collective-permute-start(bf16[4,48,512]{2,1,0:T(8,128)(2,1)S(1)} %pad_maximum_fusion.mine_ref), channel_id=1, source_target_pairs={{0,32},{32,0},{1,33},{33,1},{2,34},{34,2},{3,35},{35,3},{4,36},{36... | collective-permute-start | bytes 589832 | tf_op jit(solution)/shard_map/ppermute | solution.py:350
  14.1 16.2 %collective-permute-start.4 = (bf16[48,4096]{1,0:T(8,128)(2,1)S(1)}, bf16[48,4096]{1,0:T(8,128)(2,1)S(1)}, u32[]{:S(2)}, u32[]{:S(2)}) collective-permute-start(bf16[48,4096]{1,0:T(8,128)(2,1)S(1)} %shard_map.68.refs_0_), channel_id=1, source_target_pairs={{0,4},{4,8},{8,12},{12,16},{16,20},{20,24},{24,28},{28,0},{1,5},{5... | collective-permute-start | bytes 1179656 | tf_op jit(solution)/shard_map/ppermute | solution.py:360
  15.7 14.7 %collective-permute-start.8 = (bf16[48,4096]{1,0:T(8,128)(2,1)S(1)}, bf16[48,4096]{1,0:T(8,128)(2,1)S(1)}, u32[]{:S(2)}, u32[]{:S(2)}) collective-permute-start(bf16[48,4096]{1,0:T(8,128)(2,1)S(1)} %shard_map.68.refs_0_), channel_id=1, source_target_pairs={{0,28},{4,0},{8,4},{12,8},{16,12},{20,16},{24,20},{28,24},{1,29},{... | collective-permute-start | bytes 1179656 | tf_op jit(solution)/shard_map/ppermute | solution.py:360
  30.3 26.5 %collective-permute-start.5 = (bf16[48,4096]{1,0:T(8,128)(2,1)S(1)}, bf16[48,4096]{1,0:T(8,128)(2,1)S(1)}, u32[]{:S(2)}, u32[]{:S(2)}) collective-permute-start(bf16[48,4096]{1,0:T(8,128)(2,1)S(1)} %collective-permute-done.4.refs_0_), channel_id=1, source_target_pairs={{0,4},{4,8},{8,12},{12,16},{16,20},{20,24},{24,28},{28,0},{1,5},{5... | collective-permute-start | bytes 1179656 | tf_op jit(solution)/shard_map/ppermute | solution.py:363
  30.4 26.1 %collective-permute-start.9 = (bf16[48,4096]{1,0:T(8,128)(2,1)S(1)}, bf16[48,4096]{1,0:T(8,128)(2,1)S(1)}, u32[]{:S(2)}, u32[]{:S(2)}) collective-permute-start(bf16[48,4096]{1,0:T(8,128)(2,1)S(1)} %collective-permute-done.8.refs_1_), channel_id=1, source_target_pairs={{0,28},{4,0},{8,4},{12,8},{16,12},{20,16},{24,20},{28,24},{1,29},{... | collective-permute-start | bytes 1179656 | tf_op jit(solution)/shard_map/ppermute | solution.py:364
  56.6 25.9 %collective-permute-start.10 = (bf16[48,4096]{1,0:T(8,128)(2,1)S(1)}, bf16[48,4096]{1,0:T(8,128)(2,1)S(1)}, u32[]{:S(2)}, u32[]{:S(2)}) collective-permute-start(bf16[48,4096]{1,0:T(8,128)(2,1)S(1)} %collective-permute-done.9.refs_1_), channel_id=1, source_target_pairs={{0,28},{4,0},{8,4},{12,8},{16,12},{20,16},{24,20},{28,24},{1,29},{... | collective-permute-start | bytes 1179656 | tf_op jit(solution)/shard_map/ppermute | solution.py:364
  56.8 25.3 %collective-permute-start.6 = (bf16[48,4096]{1,0:T(8,128)(2,1)S(1)}, bf16[48,4096]{1,0:T(8,128)(2,1)S(1)}, u32[]{:S(2)}, u32[]{:S(2)}) collective-permute-start(bf16[48,4096]{1,0:T(8,128)(2,1)S(1)} %collective-permute-done.5.refs_0_), channel_id=1, source_target_pairs={{0,4},{4,8},{8,12},{12,16},{16,20},{20,24},{24,28},{28,0},{1,5},{5... | collective-permute-start | bytes 1179656 | tf_op jit(solution)/shard_map/ppermute | solution.py:363
  82.1 24.3 %collective-permute-start.7 = (bf16[48,4096]{1,0:T(8,128)(2,1)S(1)}, bf16[48,4096]{1,0:T(8,128)(2,1)S(1)}, u32[]{:S(2)}, u32[]{:S(2)}) collective-permute-start(bf16[48,4096]{1,0:T(8,128)(2,1)S(1)} %collective-permute-done.6.refs_0_), channel_id=1, source_target_pairs={{0,4},{4,8},{8,12},{12,16},{16,20},{20,24},{24,28},{28,0},{1,5},{5... | collective-permute-start | bytes 1179656 | tf_op jit(solution)/shard_map/ppermute | solution.py:363
  116.1 8.6 %collective-permute-start.11 = (f32[40,512]{1,0:T(8,128)S(1)}, f32[40,512]{1,0:T(8,128)S(1)}, u32[]{:S(2)}, u32[]{:S(2)}) collective-permute-start(f32[40,512]{1,0:T(8,128)S(1)} %get-tuple-element.40), channel_id=1, source_target_pairs={{0,1},{1,2},{2,3},{3,0},{4,5},{5,6},{6,7},{7,4},{8,9},{9,10},{10,1... | collective-permute-start | bytes 245768 | tf_op jit(solution)/shard_map/ppermute | solution.py:371
  117.4 7.3 %collective-permute-start.12 = (f32[40,512]{1,0:T(8,128)S(1)}, f32[40,512]{1,0:T(8,128)S(1)}, u32[]{:S(2)}, u32[]{:S(2)}) collective-permute-start(f32[40,512]{1,0:T(8,128)S(1)} %get-tuple-element.41), channel_id=1, source_target_pairs={{0,2},{1,3},{2,0},{3,1},{4,6},{5,7},{6,4},{7,5},{8,10},{9,11},{10,... | collective-permute-start | bytes 245768 | tf_op jit(solution)/shard_map/ppermute | solution.py:371
  120.0 4.7 %collective-permute-start.13 = (f32[40,512]{1,0:T(8,128)S(1)}, f32[40,512]{1,0:T(8,128)S(1)}, u32[]{:S(2)}, u32[]{:S(2)}) collective-permute-start(f32[40,512]{1,0:T(8,128)S(1)} %get-tuple-element.42), channel_id=1, source_target_pairs={{0,3},{1,0},{2,1},{3,2},{4,7},{5,4},{6,5},{7,6},{8,11},{9,8},{10,9... | collective-permute-start | bytes 245768 | tf_op jit(solution)/shard_map/ppermute | solution.py:371

commit v4 on v3

--- a/solution.py
+++ b/solution.py
@@ -130,7 +130,7 @@
     lax.fori_loop(0, Y, lanes_body, 0)
 
 
-def drive_kernel(*refs, shifts, earlier, parts, unroll):
+def drive_kernel(*refs, shifts, earlier, parts, pieces, unroll):
     blocks = len(shifts)
     block_refs = refs[:blocks]
     earlier_refs = refs[blocks : blocks + earlier]
@@ -163,7 +163,11 @@
         return lax.rem(lax.axis_index("y") + (parts[0] + number), Y) if parts else number
 
     def step_body(step, carry):
-        number, block = lax.shift_right_logical(step, blocks - 1), jnp.bitwise_and(step, blocks - 1)
+        if len(parts) == 1:
+            number, block = 0, step
+        else:
+            number = lax.shift_right_logical(step, blocks - 1)
+            block = jnp.bitwise_and(step, blocks - 1)
         lane = pl.multiple_of(part_at(number) * LANES, LANES)
         here = pl.ds(lane, LANES)
         if earlier == 1:
@@ -186,7 +190,7 @@
 
     total_ref[...] = earlier_refs[0][...]
     lax.fori_loop(0, (len(parts) or Y) * blocks, step_body, 0, unroll=unroll)
-    if not parts:
+    if not pieces:
         out_refs[0][...] = total_ref[...]
         return
     gram = grams_ref[0]
@@ -199,17 +203,22 @@
         out_ref[GRAM_ROW:, 128:256] = gram[4:]
 
 
-def partial_drive(shifts, blocks, earlier=(), parts=(), unroll=1):
+def partial_drive(shifts, blocks, earlier=(), parts=(), pieces=False, unroll=1):
     count = len(blocks)
     drive = jax.ShapeDtypeStruct((PAD, ROWS), jnp.float32)
-    if parts:
+    if pieces:
         out_shape = [jax.ShapeDtypeStruct((SENT, OWN), jnp.float32)] * len(parts)
     else:
         out_shape = [drive]
     grams = jax.ShapeDtypeStruct((Z, 8, 128), jnp.float32)
     return pl.pallas_call(
         functools.partial(
-            drive_kernel, shifts=shifts, earlier=len(earlier), parts=parts, unroll=unroll
+            drive_kernel,
+            shifts=shifts,
+            earlier=len(earlier),
+            parts=parts,
+            pieces=pieces,
+            unroll=unroll,
         ),
         in_specs=[VMEM] * (count + len(earlier)),
         out_specs=[VMEM] * (len(out_shape) + 1),
@@ -363,10 +372,13 @@
         next_below = lax.ppermute(below, "z", up)
         next_above = lax.ppermute(above, "z", down) if step + 1 < Z // 2 else None
         unroll = 2 if step == 1 else 1
-        earlier = partial_drive((-step, step), [below, above], earlier, unroll=unroll)
+        parts = tuple(range(1, Y)) if step + 1 == Z // 2 else ()
+        earlier = partial_drive((-step, step), [below, above], earlier, parts, unroll=unroll)
+        last = [below, above]
         below, above = next_below, next_above
-    *sent, _ = partial_drive((Z // 2,), [below], earlier, tuple(range(1, Y)))
-    kept, _ = partial_drive((Z // 2,), [below], earlier, (0,))
+    *sent, _ = partial_drive((Z // 2,), [below], earlier, tuple(range(1, Y)), pieces=True)
+    shifts = (1 - Z // 2, Z // 2 - 1, Z // 2)
+    kept, _ = partial_drive(shifts, last + [below], earlier, (0,), pieces=True)
     pieces = [kept] + [
         lax.ppermute(piece, "y", [(i, (i + shift) % Y) for i in range(Y)])
         for shift, piece in enumerate(sent, 1)

time: 158 us -> 157 us (level)
    ppermute x2, starting transfers between devices: 2.9 us -> 5.31 us  [per_device(): next_above = lax.ppermute(above, 'z', down) if step + 1 < Z // 2 else None]
where the time goes in v4:
time: 157 us
  Pallas kernels  103 us (66%)
  blocking collectives  26.9 us (17%)
  starting transfers between devices  23.9 us (15%)
    pallas_call x6, Pallas kernels, partial_drive(): pl.pallas_call(functools.partial(drive_kernel, shifts=shifts, earlier=len...  94.8 us
    all_to_all x1, blocking collectives, gather_grams(): near = jnp.sum(lax.all_to_all(copies, ('x', 'core', 'y'), 0, 0), axis=0)  14.2 us
    all_to_all x1, blocking collectives, gather_grams(): return lax.all_to_all(jnp.broadcast_to(near, (Z, *near.shape)), 'z', 0, 0)  12.7 us
    ppermute x3, starting transfers between devices, per_device(): lax.ppermute(own, 'x', [(i, (i + shift) % X) for i in range(X)])  5.72 us
    ppermute x2, starting transfers between devices, per_device(): below, above = (lax.ppermute(near, 'z', up), lax.ppermute(near, 'z', down))  5.59 us
    ppermute x2, starting transfers between devices, per_device(): next_above = lax.ppermute(above, 'z', down) if step + 1 < Z // 2 else None  5.31 us
    ppermute x3, starting transfers between devices, per_device(): lax.ppermute(piece, 'y', [(i, (i + shift) % Y) for i in range(Y)])  4.98 us
  transfers between devices with their start and end apart: 14, of which 1 were waited for; matrix products, arithmetic and copies ran while one was open for 0% of the time, Pallas kernels for 56%

profile of v4, /device:TPU:1, one launch (start us, length us, event | category | flops | bytes accessed | tf_op | source)
XLA Modules:
  0.0 156.9 jit_solution(1932570584859156345)
XLA Ops:
  2.1 2.1 %collective-permute-start = (bf16[48,512]{1,0:T(8,128)(2,1)S(1)}, bf16[48,512]{1,0:T(8,128)(2,1)S(1)}, u32[]{:S(2)}, u32[]{:S(2)}) collective-permute-start(bf16[48,512]{1,0:T(8,128)(2,1)S(1)} %shard_map.66.own_ref), channel_id=1, source_target_pairs={{0,64},{64,128},{128,192},{192,0},{1,65},{65,129},{129,193},{193,1... | collective-permute-start | bytes 147464 | tf_op jit(solution)/shard_map/ppermute | solution.py:345
  4.2 2.5 %collective-permute-start.1 = (bf16[48,512]{1,0:T(8,128)(2,1)S(1)}, bf16[48,512]{1,0:T(8,128)(2,1)S(1)}, u32[]{:S(2)}, u32[]{:S(2)}) collective-permute-start(bf16[48,512]{1,0:T(8,128)(2,1)S(1)} %shard_map.66.own_ref), channel_id=1, source_target_pairs={{0,128},{64,192},{128,0},{192,64},{1,129},{65,193},{129,1},{193,65... | collective-permute-start | bytes 147464 | tf_op jit(solution)/shard_map/ppermute | solution.py:345
  6.7 1.2 collective-permute-start.2
  7.8 2.5 %shard_map.67.refs_1_ = f32[48,2048]{1,0:T(8,128)S(1)} custom-call(s32[1,16]{1,0:T(1,128)S(1)} %copy-done.2, bf16[48,512]{1,0:T(8,128)(2,1)S(1)} %shard_map.66.own_ref), custom_call_target="tpu_custom_call" | custom-call | flops 1572864000 | bytes 49152 | tf_op jit(solution)/shard_map/pallas_call | solution.py:347
  10.4 1.8 %collective-permute-start.3 = (bf16[4,48,512]{2,1,0:T(8,128)(2,1)S(1)}, bf16[4,48,512]{2,1,0:T(8,128)(2,1)S(1)}, u32[]{:S(2)}, u32[]{:S(2)}) collective-permute-start(bf16[4,48,512]{2,1,0:T(8,128)(2,1)S(1)} %pad_maximum_fusion.mine_ref), channel_id=1, source_target_pairs={{0,32},{32,0},{1,33},{33,1},{2,34},{34,2},{3,35},{35,3},{4,36},{36... | collective-permute-start | bytes 589832 | tf_op jit(solution)/shard_map/ppermute | solution.py:359
  12.2 1.1 collective-permute-done.3.others_ref
  13.3 0.9 shard_map.68.refs_0_
  14.1 1.6 collective-permute-start.4
  15.7 4.0 %collective-permute-start.7 = (bf16[48,4096]{1,0:T(8,128)(2,1)S(1)}, bf16[48,4096]{1,0:T(8,128)(2,1)S(1)}, u32[]{:S(2)}, u32[]{:S(2)}) collective-permute-start(bf16[48,4096]{1,0:T(8,128)(2,1)S(1)} %shard_map.68.refs_0_), channel_id=1, source_target_pairs={{0,28},{4,0},{8,4},{12,8},{16,12},{20,16},{24,20},{28,24},{1,29},{... | collective-permute-start | bytes 1179656 | tf_op jit(solution)/shard_map/ppermute | solution.py:369
  19.7 10.6 %shard_map.69 = (f32[48,2048]{1,0:T(8,128)S(1)}, f32[8,8,128]{2,1,0:T(8,128)S(1)}) custom-call(bf16[48,4096]{1,0:T(8,128)(2,1)S(1)} %shard_map.68.refs_0_, f32[48,2048]{1,0:T(8,128)S(1)} %shard_map.67.refs_1_), custom_call_target="tpu_custom_call" | custom-call | flops 12582912000 | bytes 393216 | tf_op jit(solution)/shard_map/pallas_call | solution.py:214
  30.4 2.7 %collective-permute-start.8 = (bf16[48,4096]{1,0:T(8,128)(2,1)S(1)}, bf16[48,4096]{1,0:T(8,128)(2,1)S(1)}, u32[]{:S(2)}, u32[]{:S(2)}) collective-permute-start(bf16[48,4096]{1,0:T(8,128)(2,1)S(1)} %collective-permute-done.7.refs_1_), channel_id=1, source_target_pairs={{0,28},{4,0},{8,4},{12,8},{16,12},{20,16},{24,20},{28,24},{1,29},{... | collective-permute-start | bytes 1179656 | tf_op jit(solution)/shard_map/ppermute | solution.py:373
  33.1 23.4 %shard_map.70 = (f32[48,2048]{1,0:T(8,128)S(1)}, f32[8,8,128]{2,1,0:T(8,128)S(1)}) custom-call(bf16[48,4096]{1,0:T(8,128)(2,1)S(1)} %collective-permute-done.4.refs_0_, bf16[48,4096]{1,0:T(8,128)(2,1)S(1)} %collective-permute-done.7.refs_1_, f32[48,2048]{1,0:T(8,128)S(1)} %get-tuple-element.31.refs_2_, f32[8,8,128]{2,1,0:T(8,128)S(1)} %get-tuple-element.32.refs_3_), custom_call_target="tpu_custom_call" | custom-call | flops 25165824000 | bytes 786432 | tf_op jit(solution)/shard_map/pallas_call | solution.py:214
  56.7 2.7 %collective-permute-start.9 = (bf16[48,4096]{1,0:T(8,128)(2,1)S(1)}, bf16[48,4096]{1,0:T(8,128)(2,1)S(1)}, u32[]{:S(2)}, u32[]{:S(2)}) collective-permute-start(bf16[48,4096]{1,0:T(8,128)(2,1)S(1)} %collective-permute-done.8.refs_1_), channel_id=1, source_target_pairs={{0,28},{4,0},{8,4},{12,8},{16,12},{20,16},{24,20},{28,24},{1,29},{... | collective-permute-start | bytes 1179656 | tf_op jit(solution)/shard_map/ppermute | solution.py:373
  59.3 24.0 %shard_map.71 = (f32[48,2048]{1,0:T(8,128)S(1)}, f32[8,8,128]{2,1,0:T(8,128)S(1)}) custom-call(bf16[48,4096]{1,0:T(8,128)(2,1)S(1)} %collective-permute-done.5.refs_0_, bf16[48,4096]{1,0:T(8,128)(2,1)S(1)} %collective-permute-done.8.refs_1_, f32[48,2048]{1,0:T(8,128)S(1)} %get-tuple-element.33.refs_2_, f32[8,8,128]{2,1,0:T(8,128)S(1)} %get-tuple-element.34.refs_3_), custom_call_target="tpu_custom_call" | custom-call | flops 25165824000 | bytes 786432 | tf_op jit(solution)/shard_map/pallas_call | solution.py:214
  83.7 18.0 %shard_map.72 = (f32[48,2048]{1,0:T(8,128)S(1)}, f32[8,8,128]{2,1,0:T(8,128)S(1)}) custom-call(bf16[48,4096]{1,0:T(8,128)(2,1)S(1)} %collective-permute-done.6.refs_0_, bf16[48,4096]{1,0:T(8,128)(2,1)S(1)} %collective-permute-done.9.refs_1_, f32[48,2048]{1,0:T(8,128)S(1)} %get-tuple-element.35.refs_2_, f32[8,8,128]{2,1,0:T(8,128)S(1)} %get-tuple-element.36.refs_3_), custom_call_target="tpu_custom_call" | custom-call | flops 18874368000 | bytes 786432 | tf_op jit(solution)/shard_map/pallas_call | solution.py:214
  101.7 9.7 %shard_map.74 = (f32[40,512]{1,0:T(8,128)S(1)}, f32[40,512]{1,0:T(8,128)S(1)}, f32[40,512]{1,0:T(8,128)S(1)}, f32[8,8,128]{2,1,0:T(8,128)}) custom-call(bf16[48,4096]{1,0:T(8,128)(2,1)S(1)} %collective-permute-done.10.refs_2_.refs_0_, f32[48,2048]{1,0:T(8,128)S(1)} %get-tuple-element.37.refs_3_.refs_1_, f32[8,8,128]{2,1,0:T(8,128)S(1)} %get-tuple-element.38.refs_4_.refs_2_), custom_call_target="tpu_custom_call" | custom-call | flops 9437184000 | bytes 393216 | tf_op jit(solution)/shard_map/pallas_call | solution.py:214
  111.4 1.3 collective-permute-start.11
  112.7 2.6 %collective-permute-start.12 = (f32[40,512]{1,0:T(8,128)S(1)}, f32[40,512]{1,0:T(8,128)S(1)}, u32[]{:S(2)}, u32[]{:S(2)}) collective-permute-start(f32[40,512]{1,0:T(8,128)S(1)} %get-tuple-element.41), channel_id=1, source_target_pairs={{0,2},{1,3},{2,0},{3,1},{4,6},{5,7},{6,4},{7,5},{8,10},{9,11},{10,... | collective-permute-start | bytes 245768 | tf_op jit(solution)/shard_map/ppermute | solution.py:383
  115.3 1.1 collective-permute-start.13
  116.4 9.1 %shard_map.73 = (f32[40,512]{1,0:T(8,128)S(1)}, f32[8,8,128]{2,1,0:T(8,128)}) custom-call(bf16[48,4096]{1,0:T(8,128)(2,1)S(1)} %collective-permute-done.6.refs_0_, bf16[48,4096]{1,0:T(8,128)(2,1)S(1)} %collective-permute-done.9.refs_1_, bf16[48,4096]{1,0:T(8,128)(2,1)S(1)} %collective-permute-done.10.refs_2_.refs_0_, ...), custom_call_target="tpu_custom_call" | custom-call | flops 9437184000 | bytes 1179648 | tf_op jit(solution)/shard_map/pallas_call | solution.py:214
  125.5 1.8 %shard_map.75 = (f32[1,512]{1,0:T(1,128)}, f32[32,512]{1,0:T(8,128)S(1)}, f32[32,8,128]{2,1,0:T(8,128)S(1)}, f32[32,32]{1,0:T(8,128)S(1)}) custom-call(f32[40,512]{1,0:T(8,128)S(1)} %get-tuple-element.39.mine_ref, f32[40,512]{1,0:T(8,128)S(1)} %collective-permute-done.11.others_ref, f32[40,512]{1,0:T(8,128)S(1)} %collective-permute-done.12.refs_0_, ...), custom_call_target="tpu_custom_call" | custom-call | tf_op jit(solution)/shard_map/pallas_call | solution.py:389
  127.3 14.2 %all_to_all.10 = f32[32,8,128]{2,1,0:T(8,128)S(1)} all-to-all(f32[32,8,128]{2,1,0:T(8,128)S(1)} %get-tuple-element.43), channel_id=1, replica_groups=mesh['x'=4,'core'=2,'z'=8,'y'=4] {'x','core','y'}, dimensions={0} | all-to-all | bytes 262144 | tf_op jit(solution)/shard_map/all_to_all | solution.py:335
  141.5 12.7 %all_to_all.11.grams_ref = f32[8,8,128]{2,1,0:T(8,128)S(1)} all-to-all(f32[8,8,128]{2,1,0:T(8,128)S(1)} %broadcast_in_dim.3), channel_id=1, replica_groups=mesh['x'=4,'core'=2,'z'=8,'y'=4] {'z'}, dimensions={0} | all-to-all | bytes 65536 | tf_op jit(solution)/shard_map/all_to_all | solution.py:336
  154.2 2.7 %shard_map.76 = (f32[32,512]{1,0:T(8,128)}, f32[32,32]{1,0:T(8,128)}, f32[32,32]{1,0:T(8,128)}) custom-call(f32[8,8,128]{2,1,0:T(8,128)S(1)} %all_to_all.11.grams_ref, f32[32,512]{1,0:T(8,128)S(1)} %get-tuple-element.44.scaled_ref, f32[32,32]{1,0:T(8,128)S(1)} %get-tuple-element.45.input_upper_ref), custom_call_target="tpu_custom_call" | custom-call | tf_op jit(solution)/shard_map/pallas_call | solution.py:400
  (26 shorter events, 2.0 us)
Async XLA Ops:
  0.6 0.7 copy-start.1
  1.3 0.8 copy-start
  2.1 5.7 %copy-start.2 = (s32[1,16]{1,0:T(1,128)S(1)}, s32[1,16]{1,0:T(1,128)}, u32[]{:S(2)}) copy-start(s32[1,16]{1,0:T(1,128)} %keys_ref.3) | copy-start | bytes 196
  2.1 8.3 %collective-permute-start = (bf16[48,512]{1,0:T(8,128)(2,1)S(1)}, bf16[48,512]{1,0:T(8,128)(2,1)S(1)}, u32[]{:S(2)}, u32[]{:S(2)}) collective-permute-start(bf16[48,512]{1,0:T(8,128)(2,1)S(1)} %shard_map.66.own_ref), channel_id=1, source_target_pairs={{0,64},{64,128},{128,192},{192,0},{1,65},{65,129},{129,193},{193,1... | collective-permute-start | bytes 147464 | tf_op jit(solution)/shard_map/ppermute | solution.py:345
  4.2 6.2 %collective-permute-start.1 = (bf16[48,512]{1,0:T(8,128)(2,1)S(1)}, bf16[48,512]{1,0:T(8,128)(2,1)S(1)}, u32[]{:S(2)}, u32[]{:S(2)}) collective-permute-start(bf16[48,512]{1,0:T(8,128)(2,1)S(1)} %shard_map.66.own_ref), channel_id=1, source_target_pairs={{0,128},{64,192},{128,0},{192,64},{1,129},{65,193},{129,1},{193,65... | collective-permute-start | bytes 147464 | tf_op jit(solution)/shard_map/ppermute | solution.py:345
  6.7 3.7 %collective-permute-start.2 = (bf16[48,512]{1,0:T(8,128)(2,1)S(1)}, bf16[48,512]{1,0:T(8,128)(2,1)S(1)}, u32[]{:S(2)}, u32[]{:S(2)}) collective-permute-start(bf16[48,512]{1,0:T(8,128)(2,1)S(1)} %shard_map.66.own_ref), channel_id=1, source_target_pairs={{0,192},{64,0},{128,64},{192,128},{1,193},{65,1},{129,65},{193,129... | collective-permute-start | bytes 147464 | tf_op jit(solution)/shard_map/ppermute | solution.py:345
  10.4 2.9 %collective-permute-start.3 = (bf16[4,48,512]{2,1,0:T(8,128)(2,1)S(1)}, bf16[4,48,512]{2,1,0:T(8,128)(2,1)S(1)}, u32[]{:S(2)}, u32[]{:S(2)}) collective-permute-start(bf16[4,48,512]{2,1,0:T(8,128)(2,1)S(1)} %pad_maximum_fusion.mine_ref), channel_id=1, source_target_pairs={{0,32},{32,0},{1,33},{33,1},{2,34},{34,2},{3,35},{35,3},{4,36},{36... | collective-permute-start | bytes 589832 | tf_op jit(solution)/shard_map/ppermute | solution.py:359
  14.1 16.2 %collective-permute-start.4 = (bf16[48,4096]{1,0:T(8,128)(2,1)S(1)}, bf16[48,4096]{1,0:T(8,128)(2,1)S(1)}, u32[]{:S(2)}, u32[]{:S(2)}) collective-permute-start(bf16[48,4096]{1,0:T(8,128)(2,1)S(1)} %shard_map.68.refs_0_), channel_id=1, source_target_pairs={{0,4},{4,8},{8,12},{12,16},{16,20},{20,24},{24,28},{28,0},{1,5},{5... | collective-permute-start | bytes 1179656 | tf_op jit(solution)/shard_map/ppermute | solution.py:369
  15.7 14.7 %collective-permute-start.7 = (bf16[48,4096]{1,0:T(8,128)(2,1)S(1)}, bf16[48,4096]{1,0:T(8,128)(2,1)S(1)}, u32[]{:S(2)}, u32[]{:S(2)}) collective-permute-start(bf16[48,4096]{1,0:T(8,128)(2,1)S(1)} %shard_map.68.refs_0_), channel_id=1, source_target_pairs={{0,28},{4,0},{8,4},{12,8},{16,12},{20,16},{24,20},{28,24},{1,29},{... | collective-permute-start | bytes 1179656 | tf_op jit(solution)/shard_map/ppermute | solution.py:369
  30.3 26.2 %collective-permute-start.5 = (bf16[48,4096]{1,0:T(8,128)(2,1)S(1)}, bf16[48,4096]{1,0:T(8,128)(2,1)S(1)}, u32[]{:S(2)}, u32[]{:S(2)}) collective-permute-start(bf16[48,4096]{1,0:T(8,128)(2,1)S(1)} %collective-permute-done.4.refs_0_), channel_id=1, source_target_pairs={{0,4},{4,8},{8,12},{12,16},{16,20},{20,24},{24,28},{28,0},{1,5},{5... | collective-permute-start | bytes 1179656 | tf_op jit(solution)/shard_map/ppermute | solution.py:372
  30.4 26.2 %collective-permute-start.8 = (bf16[48,4096]{1,0:T(8,128)(2,1)S(1)}, bf16[48,4096]{1,0:T(8,128)(2,1)S(1)}, u32[]{:S(2)}, u32[]{:S(2)}) collective-permute-start(bf16[48,4096]{1,0:T(8,128)(2,1)S(1)} %collective-permute-done.7.refs_1_), channel_id=1, source_target_pairs={{0,28},{4,0},{8,4},{12,8},{16,12},{20,16},{24,20},{28,24},{1,29},{... | collective-permute-start | bytes 1179656 | tf_op jit(solution)/shard_map/ppermute | solution.py:373
  56.6 26.8 %collective-permute-start.6 = (bf16[48,4096]{1,0:T(8,128)(2,1)S(1)}, bf16[48,4096]{1,0:T(8,128)(2,1)S(1)}, u32[]{:S(2)}, u32[]{:S(2)}) collective-permute-start(bf16[48,4096]{1,0:T(8,128)(2,1)S(1)} %collective-permute-done.5.refs_0_), channel_id=1, source_target_pairs={{0,4},{4,8},{8,12},{12,16},{16,20},{20,24},{24,28},{28,0},{1,5},{5... | collective-permute-start | bytes 1179656 | tf_op jit(solution)/shard_map/ppermute | solution.py:372
  56.7 27.0 %collective-permute-start.9 = (bf16[48,4096]{1,0:T(8,128)(2,1)S(1)}, bf16[48,4096]{1,0:T(8,128)(2,1)S(1)}, u32[]{:S(2)}, u32[]{:S(2)}) collective-permute-start(bf16[48,4096]{1,0:T(8,128)(2,1)S(1)} %collective-permute-done.8.refs_1_), channel_id=1, source_target_pairs={{0,28},{4,0},{8,4},{12,8},{16,12},{20,16},{24,20},{28,24},{1,29},{... | collective-permute-start | bytes 1179656 | tf_op jit(solution)/shard_map/ppermute | solution.py:373
  83.3 18.4 %collective-permute-start.10 = (bf16[48,4096]{1,0:T(8,128)(2,1)S(1)}, bf16[48,4096]{1,0:T(8,128)(2,1)S(1)}, u32[]{:S(2)}, u32[]{:S(2)}) collective-permute-start(bf16[48,4096]{1,0:T(8,128)(2,1)S(1)} %collective-permute-done.6.refs_0_), channel_id=1, source_target_pairs={{0,4},{4,8},{8,12},{12,16},{16,20},{20,24},{24,28},{28,0},{1,5},{5... | collective-permute-start | bytes 1179656 | tf_op jit(solution)/shard_map/ppermute | solution.py:372
  111.4 14.1 %collective-permute-start.11 = (f32[40,512]{1,0:T(8,128)S(1)}, f32[40,512]{1,0:T(8,128)S(1)}, u32[]{:S(2)}, u32[]{:S(2)}) collective-permute-start(f32[40,512]{1,0:T(8,128)S(1)} %get-tuple-element.40), channel_id=1, source_target_pairs={{0,1},{1,2},{2,3},{3,0},{4,5},{5,6},{6,7},{7,4},{8,9},{9,10},{10,1... | collective-permute-start | bytes 245768 | tf_op jit(solution)/shard_map/ppermute | solution.py:383
  112.7 12.8 %collective-permute-start.12 = (f32[40,512]{1,0:T(8,128)S(1)}, f32[40,512]{1,0:T(8,128)S(1)}, u32[]{:S(2)}, u32[]{:S(2)}) collective-permute-start(f32[40,512]{1,0:T(8,128)S(1)} %get-tuple-element.41), channel_id=1, source_target_pairs={{0,2},{1,3},{2,0},{3,1},{4,6},{5,7},{6,4},{7,5},{8,10},{9,11},{10,... | collective-permute-start | bytes 245768 | tf_op jit(solution)/shard_map/ppermute | solution.py:383
  115.3 10.2 %collective-permute-start.13 = (f32[40,512]{1,0:T(8,128)S(1)}, f32[40,512]{1,0:T(8,128)S(1)}, u32[]{:S(2)}, u32[]{:S(2)}) collective-permute-start(f32[40,512]{1,0:T(8,128)S(1)} %get-tuple-element.42), channel_id=1, source_target_pairs={{0,3},{1,0},{2,1},{3,2},{4,7},{5,4},{6,5},{7,6},{8,11},{9,8},{10,9... | collective-permute-start | bytes 245768 | tf_op jit(solution)/shard_map/ppermute | solution.py:383

commit v5 on v4

--- a/solution.py
+++ b/solution.py
@@ -19,6 +19,7 @@
 SEG = OWN * X * CORE
 GROUP = 32
 SPARE = 40
+FROM = (0, 2, 1, 3)
 SENT = 40
 GRAM_ROW = 36
 LANES = 512
@@ -61,10 +62,10 @@
     shards_refs = (mine_ref, others_ref)
     for core in range(CORE):
         at = jnp.bitwise_xor(lax.axis_index("core"), core) * OWN
-        for shift in range(X):
+        for slot, shift in enumerate(FROM):
             chip = lax.rem(lax.axis_index("x") + (X - shift), X)
             lanes = pl.ds(pl.multiple_of(chip * (CORE * OWN) + at, OWN), OWN)
-            block_ref[:, lanes] = shards_refs[core][shift]
+            block_ref[:, lanes] = shards_refs[core][slot]
     own = block_ref[:VECS, :]
     gram = lax.dot_general(own, own, (((1,), (1,)), ((), ())), preferred_element_type=jnp.float32)
     rest = pack_gram(gram / N)
@@ -342,7 +343,7 @@
         tangent, activity.reshape(OWN // 128, 128)
     )
     shards = [
-        lax.ppermute(own, "x", [(i, (i + shift) % X) for i in range(X)]) for shift in range(1, X)
+        lax.ppermute(own, "x", [(i, (i + shift) % X) for i in range(X)]) for shift in FROM[1:]
     ]
     start = pl.pallas_call(
         shard_kernel,

time: 157 us -> 158 us (level)
  no operation moved by 1% of the time
where the time goes in v5:
time: 158 us; the launch traced here: 157 us
  Pallas kernels  103 us (65%)
  blocking collectives  26.9 us (17%)
  starting transfers between devices  24.4 us (15%)
    pallas_call x6, Pallas kernels, partial_drive(): pl.pallas_call(functools.partial(drive_kernel, shifts=shifts, earlier=len...  94.8 us
    all_to_all x1, blocking collectives, gather_grams(): near = jnp.sum(lax.all_to_all(copies, ('x', 'core', 'y'), 0, 0), axis=0)  14.3 us
    all_to_all x1, blocking collectives, gather_grams(): return lax.all_to_all(jnp.broadcast_to(near, (Z, *near.shape)), 'z', 0, 0)  12.7 us
    ppermute x3, starting transfers between devices, per_device(): lax.ppermute(own, 'x', [(i, (i + shift) % X) for i in range(X)])  6.34 us
    ppermute x2, starting transfers between devices, per_device(): below, above = (lax.ppermute(near, 'z', up), lax.ppermute(near, 'z', down))  5.7 us
    ppermute x2, starting transfers between devices, per_device(): next_above = lax.ppermute(above, 'z', down) if step + 1 < Z // 2 else None  5.31 us
    ppermute x3, starting transfers between devices, per_device(): lax.ppermute(piece, 'y', [(i, (i + shift) % Y) for i in range(Y)])  4.98 us
  transfers between devices with their start and end apart: 14, of which 1 were waited for; matrix products, arithmetic and copies ran while one was open for 0% of the time, Pallas kernels for 56%

profile of v5, /device:TPU:1, one launch (start us, length us, event | category | flops | bytes accessed | tf_op | source)
XLA Modules:
  0.0 157.5 jit_solution(12143374106946020953)
XLA Ops:
  1.3 0.8 copy-done
  2.1 3.7 %collective-permute-start = (bf16[48,512]{1,0:T(8,128)(2,1)S(1)}, bf16[48,512]{1,0:T(8,128)(2,1)S(1)}, u32[]{:S(2)}, u32[]{:S(2)}) collective-permute-start(bf16[48,512]{1,0:T(8,128)(2,1)S(1)} %shard_map.66.own_ref), channel_id=1, source_target_pairs={{0,128},{64,192},{128,0},{192,64},{1,129},{65,193},{129,1},{193,65... | collective-permute-start | bytes 147464 | tf_op jit(solution)/shard_map/ppermute | solution.py:346
  6.1 2.4 %collective-permute-start.2 = (bf16[48,512]{1,0:T(8,128)(2,1)S(1)}, bf16[48,512]{1,0:T(8,128)(2,1)S(1)}, u32[]{:S(2)}, u32[]{:S(2)}) collective-permute-start(bf16[48,512]{1,0:T(8,128)(2,1)S(1)} %shard_map.66.own_ref), channel_id=1, source_target_pairs={{0,192},{64,0},{128,64},{192,128},{1,193},{65,1},{129,65},{193,129... | collective-permute-start | bytes 147464 | tf_op jit(solution)/shard_map/ppermute | solution.py:346
  8.4 2.5 %shard_map.67.refs_1_ = f32[48,2048]{1,0:T(8,128)S(1)} custom-call(s32[1,16]{1,0:T(1,128)S(1)} %copy-done.2, bf16[48,512]{1,0:T(8,128)(2,1)S(1)} %shard_map.66.own_ref), custom_call_target="tpu_custom_call" | custom-call | flops 1572864000 | bytes 49152 | tf_op jit(solution)/shard_map/pallas_call | solution.py:348
  11.0 1.6 %collective-permute-start.3 = (bf16[4,48,512]{2,1,0:T(8,128)(2,1)S(1)}, bf16[4,48,512]{2,1,0:T(8,128)(2,1)S(1)}, u32[]{:S(2)}, u32[]{:S(2)}) collective-permute-start(bf16[4,48,512]{2,1,0:T(8,128)(2,1)S(1)} %pad_maximum_fusion.mine_ref), channel_id=1, source_target_pairs={{0,32},{32,0},{1,33},{33,1},{2,34},{34,2},{3,35},{35,3},{4,36},{36... | collective-permute-start | bytes 589832 | tf_op jit(solution)/shard_map/ppermute | solution.py:360
  12.6 1.1 collective-permute-done.3.others_ref
  13.7 0.9 shard_map.68.refs_0_
  14.6 1.7 %collective-permute-start.4 = (bf16[48,4096]{1,0:T(8,128)(2,1)S(1)}, bf16[48,4096]{1,0:T(8,128)(2,1)S(1)}, u32[]{:S(2)}, u32[]{:S(2)}) collective-permute-start(bf16[48,4096]{1,0:T(8,128)(2,1)S(1)} %shard_map.68.refs_0_), channel_id=1, source_target_pairs={{0,4},{4,8},{8,12},{12,16},{16,20},{20,24},{24,28},{28,0},{1,5},{5... | collective-permute-start | bytes 1179656 | tf_op jit(solution)/shard_map/ppermute | solution.py:370
  16.2 4.0 %collective-permute-start.7 = (bf16[48,4096]{1,0:T(8,128)(2,1)S(1)}, bf16[48,4096]{1,0:T(8,128)(2,1)S(1)}, u32[]{:S(2)}, u32[]{:S(2)}) collective-permute-start(bf16[48,4096]{1,0:T(8,128)(2,1)S(1)} %shard_map.68.refs_0_), channel_id=1, source_target_pairs={{0,28},{4,0},{8,4},{12,8},{16,12},{20,16},{24,20},{28,24},{1,29},{... | collective-permute-start | bytes 1179656 | tf_op jit(solution)/shard_map/ppermute | solution.py:370
  20.3 10.6 %shard_map.69 = (f32[48,2048]{1,0:T(8,128)S(1)}, f32[8,8,128]{2,1,0:T(8,128)S(1)}) custom-call(bf16[48,4096]{1,0:T(8,128)(2,1)S(1)} %shard_map.68.refs_0_, f32[48,2048]{1,0:T(8,128)S(1)} %shard_map.67.refs_1_), custom_call_target="tpu_custom_call" | custom-call | flops 12582912000 | bytes 393216 | tf_op jit(solution)/shard_map/pallas_call | solution.py:215
  31.0 2.7 %collective-permute-start.8 = (bf16[48,4096]{1,0:T(8,128)(2,1)S(1)}, bf16[48,4096]{1,0:T(8,128)(2,1)S(1)}, u32[]{:S(2)}, u32[]{:S(2)}) collective-permute-start(bf16[48,4096]{1,0:T(8,128)(2,1)S(1)} %collective-permute-done.7.refs_1_), channel_id=1, source_target_pairs={{0,28},{4,0},{8,4},{12,8},{16,12},{20,16},{24,20},{28,24},{1,29},{... | collective-permute-start | bytes 1179656 | tf_op jit(solution)/shard_map/ppermute | solution.py:374
  33.6 23.4 %shard_map.70 = (f32[48,2048]{1,0:T(8,128)S(1)}, f32[8,8,128]{2,1,0:T(8,128)S(1)}) custom-call(bf16[48,4096]{1,0:T(8,128)(2,1)S(1)} %collective-permute-done.4.refs_0_, bf16[48,4096]{1,0:T(8,128)(2,1)S(1)} %collective-permute-done.7.refs_1_, f32[48,2048]{1,0:T(8,128)S(1)} %get-tuple-element.31.refs_2_, f32[8,8,128]{2,1,0:T(8,128)S(1)} %get-tuple-element.32.refs_3_), custom_call_target="tpu_custom_call" | custom-call | flops 25165824000 | bytes 786432 | tf_op jit(solution)/shard_map/pallas_call | solution.py:215
  57.2 2.7 %collective-permute-start.9 = (bf16[48,4096]{1,0:T(8,128)(2,1)S(1)}, bf16[48,4096]{1,0:T(8,128)(2,1)S(1)}, u32[]{:S(2)}, u32[]{:S(2)}) collective-permute-start(bf16[48,4096]{1,0:T(8,128)(2,1)S(1)} %collective-permute-done.8.refs_1_), channel_id=1, source_target_pairs={{0,28},{4,0},{8,4},{12,8},{16,12},{20,16},{24,20},{28,24},{1,29},{... | collective-permute-start | bytes 1179656 | tf_op jit(solution)/shard_map/ppermute | solution.py:374
  59.9 24.0 %shard_map.71 = (f32[48,2048]{1,0:T(8,128)S(1)}, f32[8,8,128]{2,1,0:T(8,128)S(1)}) custom-call(bf16[48,4096]{1,0:T(8,128)(2,1)S(1)} %collective-permute-done.5.refs_0_, bf16[48,4096]{1,0:T(8,128)(2,1)S(1)} %collective-permute-done.8.refs_1_, f32[48,2048]{1,0:T(8,128)S(1)} %get-tuple-element.33.refs_2_, f32[8,8,128]{2,1,0:T(8,128)S(1)} %get-tuple-element.34.refs_3_), custom_call_target="tpu_custom_call" | custom-call | flops 25165824000 | bytes 786432 | tf_op jit(solution)/shard_map/pallas_call | solution.py:215
  84.2 18.0 %shard_map.72 = (f32[48,2048]{1,0:T(8,128)S(1)}, f32[8,8,128]{2,1,0:T(8,128)S(1)}) custom-call(bf16[48,4096]{1,0:T(8,128)(2,1)S(1)} %collective-permute-done.6.refs_0_, bf16[48,4096]{1,0:T(8,128)(2,1)S(1)} %collective-permute-done.9.refs_1_, f32[48,2048]{1,0:T(8,128)S(1)} %get-tuple-element.35.refs_2_, f32[8,8,128]{2,1,0:T(8,128)S(1)} %get-tuple-element.36.refs_3_), custom_call_target="tpu_custom_call" | custom-call | flops 18874368000 | bytes 786432 | tf_op jit(solution)/shard_map/pallas_call | solution.py:215
  102.2 9.7 %shard_map.74 = (f32[40,512]{1,0:T(8,128)S(1)}, f32[40,512]{1,0:T(8,128)S(1)}, f32[40,512]{1,0:T(8,128)S(1)}, f32[8,8,128]{2,1,0:T(8,128)}) custom-call(bf16[48,4096]{1,0:T(8,128)(2,1)S(1)} %collective-permute-done.10.refs_2_.refs_0_, f32[48,2048]{1,0:T(8,128)S(1)} %get-tuple-element.37.refs_3_.refs_1_, f32[8,8,128]{2,1,0:T(8,128)S(1)} %get-tuple-element.38.refs_4_.refs_2_), custom_call_target="tpu_custom_call" | custom-call | flops 9437184000 | bytes 393216 | tf_op jit(solution)/shard_map/pallas_call | solution.py:215
  111.9 1.3 collective-permute-start.11
  113.2 2.6 %collective-permute-start.12 = (f32[40,512]{1,0:T(8,128)S(1)}, f32[40,512]{1,0:T(8,128)S(1)}, u32[]{:S(2)}, u32[]{:S(2)}) collective-permute-start(f32[40,512]{1,0:T(8,128)S(1)} %get-tuple-element.41), channel_id=1, source_target_pairs={{0,2},{1,3},{2,0},{3,1},{4,6},{5,7},{6,4},{7,5},{8,10},{9,11},{10,... | collective-permute-start | bytes 245768 | tf_op jit(solution)/shard_map/ppermute | solution.py:384
  115.8 1.1 collective-permute-start.13
  116.9 9.1 %shard_map.73 = (f32[40,512]{1,0:T(8,128)S(1)}, f32[8,8,128]{2,1,0:T(8,128)}) custom-call(bf16[48,4096]{1,0:T(8,128)(2,1)S(1)} %collective-permute-done.6.refs_0_, bf16[48,4096]{1,0:T(8,128)(2,1)S(1)} %collective-permute-done.9.refs_1_, bf16[48,4096]{1,0:T(8,128)(2,1)S(1)} %collective-permute-done.10.refs_2_.refs_0_, ...), custom_call_target="tpu_custom_call" | custom-call | flops 9437184000 | bytes 1179648 | tf_op jit(solution)/shard_map/pallas_call | solution.py:215
  126.0 1.8 %shard_map.75 = (f32[1,512]{1,0:T(1,128)}, f32[32,512]{1,0:T(8,128)S(1)}, f32[32,8,128]{2,1,0:T(8,128)S(1)}, f32[32,32]{1,0:T(8,128)S(1)}) custom-call(f32[40,512]{1,0:T(8,128)S(1)} %get-tuple-element.39.mine_ref, f32[40,512]{1,0:T(8,128)S(1)} %collective-permute-done.11.others_ref, f32[40,512]{1,0:T(8,128)S(1)} %collective-permute-done.12.refs_0_, ...), custom_call_target="tpu_custom_call" | custom-call | tf_op jit(solution)/shard_map/pallas_call | solution.py:390
  127.8 14.3 %all_to_all.10 = f32[32,8,128]{2,1,0:T(8,128)S(1)} all-to-all(f32[32,8,128]{2,1,0:T(8,128)S(1)} %get-tuple-element.43), channel_id=1, replica_groups=mesh['x'=4,'core'=2,'z'=8,'y'=4] {'x','core','y'}, dimensions={0} | all-to-all | bytes 262144 | tf_op jit(solution)/shard_map/all_to_all | solution.py:336
  142.1 12.7 %all_to_all.11.grams_ref = f32[8,8,128]{2,1,0:T(8,128)S(1)} all-to-all(f32[8,8,128]{2,1,0:T(8,128)S(1)} %broadcast_in_dim.3), channel_id=1, replica_groups=mesh['x'=4,'core'=2,'z'=8,'y'=4] {'z'}, dimensions={0} | all-to-all | bytes 65536 | tf_op jit(solution)/shard_map/all_to_all | solution.py:337
  154.8 2.7 %shard_map.76 = (f32[32,512]{1,0:T(8,128)}, f32[32,32]{1,0:T(8,128)}, f32[32,32]{1,0:T(8,128)}) custom-call(f32[8,8,128]{2,1,0:T(8,128)S(1)} %all_to_all.11.grams_ref, f32[32,512]{1,0:T(8,128)S(1)} %get-tuple-element.44.scaled_ref, f32[32,32]{1,0:T(8,128)S(1)} %get-tuple-element.45.input_upper_ref), custom_call_target="tpu_custom_call" | custom-call | tf_op jit(solution)/shard_map/pallas_call | solution.py:401
  (26 shorter events, 1.6 us)
Async XLA Ops:
  0.6 0.7 copy-start.1
  1.3 0.8 copy-start
  2.1 6.4 %copy-start.2 = (s32[1,16]{1,0:T(1,128)S(1)}, s32[1,16]{1,0:T(1,128)}, u32[]{:S(2)}) copy-start(s32[1,16]{1,0:T(1,128)} %keys_ref.3) | copy-start | bytes 196
  2.1 8.9 %collective-permute-start = (bf16[48,512]{1,0:T(8,128)(2,1)S(1)}, bf16[48,512]{1,0:T(8,128)(2,1)S(1)}, u32[]{:S(2)}, u32[]{:S(2)}) collective-permute-start(bf16[48,512]{1,0:T(8,128)(2,1)S(1)} %shard_map.66.own_ref), channel_id=1, source_target_pairs={{0,128},{64,192},{128,0},{192,64},{1,129},{65,193},{129,1},{193,65... | collective-permute-start | bytes 147464 | tf_op jit(solution)/shard_map/ppermute | solution.py:346
  5.7 5.2 %collective-permute-start.1 = (bf16[48,512]{1,0:T(8,128)(2,1)S(1)}, bf16[48,512]{1,0:T(8,128)(2,1)S(1)}, u32[]{:S(2)}, u32[]{:S(2)}) collective-permute-start(bf16[48,512]{1,0:T(8,128)(2,1)S(1)} %shard_map.66.own_ref), channel_id=1, source_target_pairs={{0,64},{64,128},{128,192},{192,0},{1,65},{65,129},{129,193},{193,1... | collective-permute-start | bytes 147464 | tf_op jit(solution)/shard_map/ppermute | solution.py:346
  6.1 4.9 %collective-permute-start.2 = (bf16[48,512]{1,0:T(8,128)(2,1)S(1)}, bf16[48,512]{1,0:T(8,128)(2,1)S(1)}, u32[]{:S(2)}, u32[]{:S(2)}) collective-permute-start(bf16[48,512]{1,0:T(8,128)(2,1)S(1)} %shard_map.66.own_ref), channel_id=1, source_target_pairs={{0,192},{64,0},{128,64},{192,128},{1,193},{65,1},{129,65},{193,129... | collective-permute-start | bytes 147464 | tf_op jit(solution)/shard_map/ppermute | solution.py:346
  11.0 2.7 %collective-permute-start.3 = (bf16[4,48,512]{2,1,0:T(8,128)(2,1)S(1)}, bf16[4,48,512]{2,1,0:T(8,128)(2,1)S(1)}, u32[]{:S(2)}, u32[]{:S(2)}) collective-permute-start(bf16[4,48,512]{2,1,0:T(8,128)(2,1)S(1)} %pad_maximum_fusion.mine_ref), channel_id=1, source_target_pairs={{0,32},{32,0},{1,33},{33,1},{2,34},{34,2},{3,35},{35,3},{4,36},{36... | collective-permute-start | bytes 589832 | tf_op jit(solution)/shard_map/ppermute | solution.py:360
  14.6 16.3 %collective-permute-start.4 = (bf16[48,4096]{1,0:T(8,128)(2,1)S(1)}, bf16[48,4096]{1,0:T(8,128)(2,1)S(1)}, u32[]{:S(2)}, u32[]{:S(2)}) collective-permute-start(bf16[48,4096]{1,0:T(8,128)(2,1)S(1)} %shard_map.68.refs_0_), channel_id=1, source_target_pairs={{0,4},{4,8},{8,12},{12,16},{16,20},{20,24},{24,28},{28,0},{1,5},{5... | collective-permute-start | bytes 1179656 | tf_op jit(solution)/shard_map/ppermute | solution.py:370
  16.2 14.7 %collective-permute-start.7 = (bf16[48,4096]{1,0:T(8,128)(2,1)S(1)}, bf16[48,4096]{1,0:T(8,128)(2,1)S(1)}, u32[]{:S(2)}, u32[]{:S(2)}) collective-permute-start(bf16[48,4096]{1,0:T(8,128)(2,1)S(1)} %shard_map.68.refs_0_), channel_id=1, source_target_pairs={{0,28},{4,0},{8,4},{12,8},{16,12},{20,16},{24,20},{28,24},{1,29},{... | collective-permute-start | bytes 1179656 | tf_op jit(solution)/shard_map/ppermute | solution.py:370
  30.9 26.2 %collective-permute-start.5 = (bf16[48,4096]{1,0:T(8,128)(2,1)S(1)}, bf16[48,4096]{1,0:T(8,128)(2,1)S(1)}, u32[]{:S(2)}, u32[]{:S(2)}) collective-permute-start(bf16[48,4096]{1,0:T(8,128)(2,1)S(1)} %collective-permute-done.4.refs_0_), channel_id=1, source_target_pairs={{0,4},{4,8},{8,12},{12,16},{16,20},{20,24},{24,28},{28,0},{1,5},{5... | collective-permute-start | bytes 1179656 | tf_op jit(solution)/shard_map/ppermute | solution.py:373
  31.0 26.2 %collective-permute-start.8 = (bf16[48,4096]{1,0:T(8,128)(2,1)S(1)}, bf16[48,4096]{1,0:T(8,128)(2,1)S(1)}, u32[]{:S(2)}, u32[]{:S(2)}) collective-permute-start(bf16[48,4096]{1,0:T(8,128)(2,1)S(1)} %collective-permute-done.7.refs_1_), channel_id=1, source_target_pairs={{0,28},{4,0},{8,4},{12,8},{16,12},{20,16},{24,20},{28,24},{1,29},{... | collective-permute-start | bytes 1179656 | tf_op jit(solution)/shard_map/ppermute | solution.py:374
  57.1 26.8 %collective-permute-start.6 = (bf16[48,4096]{1,0:T(8,128)(2,1)S(1)}, bf16[48,4096]{1,0:T(8,128)(2,1)S(1)}, u32[]{:S(2)}, u32[]{:S(2)}) collective-permute-start(bf16[48,4096]{1,0:T(8,128)(2,1)S(1)} %collective-permute-done.5.refs_0_), channel_id=1, source_target_pairs={{0,4},{4,8},{8,12},{12,16},{16,20},{20,24},{24,28},{28,0},{1,5},{5... | collective-permute-start | bytes 1179656 | tf_op jit(solution)/shard_map/ppermute | solution.py:373
  57.2 27.0 %collective-permute-start.9 = (bf16[48,4096]{1,0:T(8,128)(2,1)S(1)}, bf16[48,4096]{1,0:T(8,128)(2,1)S(1)}, u32[]{:S(2)}, u32[]{:S(2)}) collective-permute-start(bf16[48,4096]{1,0:T(8,128)(2,1)S(1)} %collective-permute-done.8.refs_1_), channel_id=1, source_target_pairs={{0,28},{4,0},{8,4},{12,8},{16,12},{20,16},{24,20},{28,24},{1,29},{... | collective-permute-start | bytes 1179656 | tf_op jit(solution)/shard_map/ppermute | solution.py:374
  83.9 18.4 %collective-permute-start.10 = (bf16[48,4096]{1,0:T(8,128)(2,1)S(1)}, bf16[48,4096]{1,0:T(8,128)(2,1)S(1)}, u32[]{:S(2)}, u32[]{:S(2)}) collective-permute-start(bf16[48,4096]{1,0:T(8,128)(2,1)S(1)} %collective-permute-done.6.refs_0_), channel_id=1, source_target_pairs={{0,4},{4,8},{8,12},{12,16},{16,20},{20,24},{24,28},{28,0},{1,5},{5... | collective-permute-start | bytes 1179656 | tf_op jit(solution)/shard_map/ppermute | solution.py:373
  111.9 14.1 %collective-permute-start.11 = (f32[40,512]{1,0:T(8,128)S(1)}, f32[40,512]{1,0:T(8,128)S(1)}, u32[]{:S(2)}, u32[]{:S(2)}) collective-permute-start(f32[40,512]{1,0:T(8,128)S(1)} %get-tuple-element.40), channel_id=1, source_target_pairs={{0,1},{1,2},{2,3},{3,0},{4,5},{5,6},{6,7},{7,4},{8,9},{9,10},{10,1... | collective-permute-start | bytes 245768 | tf_op jit(solution)/shard_map/ppermute | solution.py:384
  113.2 12.8 %collective-permute-start.12 = (f32[40,512]{1,0:T(8,128)S(1)}, f32[40,512]{1,0:T(8,128)S(1)}, u32[]{:S(2)}, u32[]{:S(2)}) collective-permute-start(f32[40,512]{1,0:T(8,128)S(1)} %get-tuple-element.41), channel_id=1, source_target_pairs={{0,2},{1,3},{2,0},{3,1},{4,6},{5,7},{6,4},{7,5},{8,10},{9,11},{10,... | collective-permute-start | bytes 245768 | tf_op jit(solution)/shard_map/ppermute | solution.py:384
  115.8 10.2 %collective-permute-start.13 = (f32[40,512]{1,0:T(8,128)S(1)}, f32[40,512]{1,0:T(8,128)S(1)}, u32[]{:S(2)}, u32[]{:S(2)}) collective-permute-start(f32[40,512]{1,0:T(8,128)S(1)} %get-tuple-element.42), channel_id=1, source_target_pairs={{0,3},{1,0},{2,1},{3,2},{4,7},{5,4},{6,5},{7,6},{8,11},{9,8},{10,9... | collective-permute-start | bytes 245768 | tf_op jit(solution)/shard_map/ppermute | solution.py:384
